TPU v7x, 32 devices: a whole 2x2x4 slice. The times are simulated.
32 devices in a mesh: col: 16 (over z, x, core), tm: 2 (over y).
Axes of the slice: x: 2, y: 2, z: 4, core: 2. Of those that a mesh axis runs over, the one named last changes fastest.
Arguments:
- series: bfloat16 [1200, 24576], P(None, 'col'), may hold values from -700 to 700
- slab_series: float32 [1200, 512], P('tm', 'col'), may hold values from -700 to 700
- phase_index: int32 [4, 600], P(None, 'tm'), may hold values from 0 to 1199
Outputs:
- tile_peak: float32 [4, 512, 16], P(None, None, 'col')
- peak_all: float32 [4], replicated
All inputs are finite; a program needn't handle non-finite values.
Results may differ from a plain program's by a relative error of at most 0.0013.
Values may be sent and summed in bfloat16 or wider, within the bound.
No kernel may reach another device: no remote copies, remote signals or barrier semaphores. Data moves between devices by JAX's collectives and lax.ppermute only.
A program may use at most 64 MiB of HBM per device.

v0:
```python
import functools
import math

import jax
import jax.numpy as jnp
import ml_dtypes
import numpy as np
from jax import lax
from jax.experimental import pallas as pl
from jax.experimental.pallas import tpu as pltpu
from jax.sharding import Mesh, PartitionSpec as P

EPSILON = 1e-06
LANES = 128
CODE_TOP = 32767.0
VMEM = pl.BlockSpec(memory_space=pltpu.VMEM)


def round_up(value, unit):
    return -(-value // unit) * unit


def dft_tables(frames, freqs, n_tm):
    share = frames // n_tm
    share_pad = round_up(share, LANES)
    freq_pad = round_up(freqs, LANES)
    turns = np.arange(1, freqs + 1)[:, None] * np.arange(frames)[None, :] % frames
    angles = turns * (2.0 * math.pi / frames)
    table = np.zeros((2, freq_pad, n_tm, share_pad), np.float64)
    table[0, :freqs, :, :share] = np.cos(angles).reshape(freqs, n_tm, share)
    table[1, :freqs, :, :share] = np.sin(angles).reshape(freqs, n_tm, share)
    block_sums = table.sum(axis=3).transpose(2, 0, 1).reshape(n_tm, 1, 2 * freq_pad)
    table = table.reshape(2 * freq_pad, n_tm * share_pad)
    high = table.astype(ml_dtypes.bfloat16)
    low = (table - high.astype(np.float64)).astype(ml_dtypes.bfloat16)
    return high, low, block_sums.astype(np.float32)


def split_digits(value):
    scaled = value * 16.0
    first = scaled.astype(jnp.int32)
    rest = (scaled - first.astype(jnp.float32)) * 32768.0
    second = rest.astype(jnp.int32)
    third = ((rest - second.astype(jnp.float32)) * 32768.0).astype(jnp.int32)
    return first, second, third


def join_digits(first, second, third):
    return (
        first.astype(jnp.float32) * 2.0**-4
        + second.astype(jnp.float32) * 2.0**-19
        + third.astype(jnp.float32) * 2.0**-34
    )


def encode_kernel(share, slab_ref, code_ref):
    values = slab_ref[...]
    verts = values.shape[0]
    n_tm, n_grp, row_share, share_pad = code_ref.shape
    mean = jnp.sum(values, axis=1, keepdims=True) * (1.0 / share)
    offset = values - mean
    top = jnp.max(jnp.abs(offset), axis=1, keepdims=True)
    top_digits = split_digits(top)
    mean_digits = split_digits(mean)
    step = join_digits(*top_digits) * (1.0 / CODE_TOP)
    inverse = jnp.where(step > 0.0, 1.0 / jnp.where(step > 0.0, step, 1.0), 0.0)
    codes = jnp.clip(jnp.round(offset * inverse), -CODE_TOP, CODE_TOP).astype(jnp.int32)
    codes = jnp.concatenate(
        [codes, jnp.zeros((verts, share_pad - share), jnp.int32)], axis=1
    )
    lane = lax.broadcasted_iota(jnp.int32, (verts, share_pad), 1) - share
    for place, digit in enumerate(top_digits + mean_digits):
        codes = jnp.where(lane == place, digit, codes)
    for m in range(n_tm):
        block = codes[m * row_share : (m + 1) * row_share].astype(jnp.int16)
        for g in range(n_grp):
            code_ref[m, g] = block


def column_kernel(share, share_pad, series_ref, high_ref, low_ref, out_ref, normed_ref):
    values = series_ref[...].astype(jnp.float32)
    frames = values.shape[0]
    centered = values - jnp.sum(values, axis=0, keepdims=True) * (1.0 / frames)
    total = jnp.sum(centered * centered, axis=0, keepdims=True)
    normed = centered * lax.rsqrt(total + EPSILON)
    gap = share_pad - share
    for m in range(frames // share):
        normed_ref[pl.ds(m * share_pad, share), :] = normed[m * share : (m + 1) * share].astype(
            jnp.bfloat16
        )
        if gap:
            normed_ref[pl.ds(m * share_pad + share, gap), :] = jnp.zeros(
                (gap, values.shape[1]), jnp.bfloat16
            )
    tile = normed_ref[...]
    out = jnp.dot(high_ref[...], tile, preferred_element_type=jnp.float32)
    out += jnp.dot(low_ref[...], tile, preferred_element_type=jnp.float32)
    out_ref[...] = out.astype(jnp.bfloat16)


def dot_nt(left, right):
    return lax.dot_general(
        left, right, (((1,), (1,)), ((), ())), preferred_element_type=jnp.float32
    )


def score_kernel(
    sizes, code_ref, high_ref, low_ref, sums_ref, turn_ref, cols_ref, peak_ref, rot_ref
):
    share, frames, freqs, surr = sizes
    n_tm, rows, share_pad = code_ref.shape
    freq_pad = turn_ref.shape[1]
    spec = jnp.zeros((rows, 2 * freq_pad), jnp.float32)
    for m in range(n_tm):
        codes = code_ref[m].astype(jnp.int32)
        upper = ((codes + 128) >> 8) << 8
        lower = codes - upper
        upper = upper.astype(jnp.float32).astype(jnp.bfloat16)
        lower = lower.astype(jnp.float32).astype(jnp.bfloat16)
        digits = [codes[:, share + p : share + p + 1] for p in range(6)]
        step = join_digits(*digits[:3]) * (1.0 / CODE_TOP)
        mean = join_digits(*digits[3:])
        block = pl.ds(m * share_pad, share_pad)
        high = high_ref[:, block]
        part = dot_nt(upper, high) + dot_nt(lower, high) + dot_nt(upper, low_ref[:, block])
        spec = spec + part * step + mean * sums_ref[m]
    spec_cos = spec[:, :freq_pad]
    spec_sin = spec[:, freq_pad:]
    freq = lax.broadcasted_iota(jnp.int32, (1, freq_pad), 1)
    pair = jnp.where(freq < freqs - 1, (2.0 / frames) ** 2 * (frames / 2.0), 0.0)
    last = jnp.where(freq == freqs - 1, float(frames), 0.0)
    common = jnp.sum((spec_cos * spec_cos + spec_sin * spec_sin) * pair, axis=1, keepdims=True)
    inverse = []
    for s in range(surr):
        cos_row = turn_ref[pl.ds(s, 1), :]
        sin_row = turn_ref[pl.ds(surr + s, 1), :]
        rot_real = spec_cos * cos_row + spec_sin * sin_row
        rot_imag = spec_cos * sin_row - spec_sin * cos_row
        energy = common + jnp.sum(rot_real * rot_real * last, axis=1, keepdims=True)
        inverse.append(lax.rsqrt(energy + EPSILON) * math.sqrt(frames))
        span = pl.ds(s * rows, rows)
        rot_ref[span, :freq_pad] = rot_real.astype(jnp.bfloat16)
        rot_ref[span, freq_pad:] = (-rot_imag).astype(jnp.bfloat16)
    rot = rot_ref[...]
    width = cols_ref.shape[1]
    step_cols = 2 * LANES
    top = jnp.zeros((surr * rows, LANES), jnp.float32)
    for start in range(0, width, step_cols):
        scores = jnp.abs(
            jnp.dot(rot, cols_ref[:, pl.ds(start, step_cols)], preferred_element_type=jnp.float32)
        )
        for part in range(0, step_cols, LANES):
            top = jnp.maximum(top, scores[:, part : part + LANES])
    for s in range(surr):
        scaled = top[s * rows : (s + 1) * rows] * inverse[s]
        peak_ref[pl.ds(s, 1), :] = jnp.max(scaled.T, axis=0, keepdims=True)


def tm_exchange(value, n_tm):
    if n_tm == 2:
        other = lax.ppermute(value, "tm", [(0, 1), (1, 0)])
        first = lax.axis_index("tm") == 0
        return jnp.stack([jnp.where(first, value, other), jnp.where(first, other, value)])
    return lax.all_gather(value, "tm")


def body(dims, series, slab_series, phase_index):
    n_grp, n_lane, n_tm = dims
    frames, columns = series.shape
    share, verts = slab_series.shape
    surr = phase_index.shape[0]
    freqs = phase_index.shape[1] * n_tm
    row_share = verts // n_tm
    rows = n_grp * row_share
    share_pad = round_up(share, LANES)
    freq_pad = round_up(freqs, LANES)
    high, low, sums = (jnp.asarray(t) for t in dft_tables(frames, freqs, n_tm))

    codes = pl.pallas_call(
        functools.partial(encode_kernel, share),
        out_shape=jax.ShapeDtypeStruct((n_tm, n_grp, row_share, share_pad), jnp.int16),
        in_specs=[VMEM],
        out_specs=VMEM,
    )(slab_series.T)
    codes = codes.reshape(n_tm * n_grp, row_share, share_pad)
    received = lax.all_to_all(codes, ("tm", "grp"), 0, 0, tiled=True)

    phase = tm_exchange(phase_index, n_tm)
    phase = jnp.transpose(phase, (1, 0, 2)).reshape(surr, freqs)
    angle = phase.astype(jnp.float32) * (2.0 * math.pi / frames)
    weight = jnp.where(jnp.arange(1, freqs + 1) < freqs, 2.0, 1.0) / frames
    turn = jnp.concatenate([jnp.cos(angle) * weight, jnp.sin(angle) * weight], axis=0)
    turn = jnp.pad(turn, ((0, 0), (0, freq_pad - freqs)))

    tile = 2 * LANES
    cols = pl.pallas_call(
        functools.partial(column_kernel, share, share_pad),
        out_shape=jax.ShapeDtypeStruct((2 * freq_pad, columns), jnp.bfloat16),
        grid=(columns // tile,),
        in_specs=[pl.BlockSpec((frames, tile), lambda j: (0, j)), VMEM, VMEM],
        out_specs=pl.BlockSpec((2 * freq_pad, tile), lambda j: (0, j)),
        scratch_shapes=[pltpu.VMEM((n_tm * share_pad, tile), jnp.bfloat16)],
        compiler_params=pltpu.CompilerParams(vmem_limit_bytes=40 * 2**20),
    )(series, high, low)

    received, cols = lax.optimization_barrier((received, cols))
    lanes = [received]
    if n_lane == 2:
        lanes.append(lax.ppermute(received, "lane", [(0, 1), (1, 0)]))
    score = pl.pallas_call(
        functools.partial(score_kernel, (share, frames, freqs, surr)),
        out_shape=jax.ShapeDtypeStruct((surr, rows), jnp.float32),
        in_specs=[VMEM] * 6,
        out_specs=VMEM,
        scratch_shapes=[pltpu.VMEM((surr * rows, 2 * freq_pad), jnp.bfloat16)],
        compiler_params=pltpu.CompilerParams(vmem_limit_bytes=40 * 2**20),
    )
    peaks = [
        score(r.reshape(n_tm, rows, share_pad), high, low, sums, turn, cols) for r in lanes
    ]

    best = functools.reduce(jnp.maximum, peaks)
    n_dev = n_grp * n_lane * n_tm
    every = lax.all_to_all(
        jnp.broadcast_to(best, (n_dev, surr, rows)), ("grp", "lane", "tm"), 0, 0, tiled=True
    )
    peak_all = jnp.max(every, axis=(0, 2))

    if n_lane == 2:
        first = lax.axis_index("lane") == 0
        peaks = [jnp.where(first, peaks[0], peaks[1]), jnp.where(first, peaks[1], peaks[0])]
    own = jnp.stack(peaks)
    both = tm_exchange(own, n_tm).reshape(n_tm, n_lane, surr, n_grp, row_share)
    tile_peak = jnp.transpose(both, (2, 3, 1, 0, 4)).reshape(surr, -1, 1)
    return tile_peak, peak_all


def solution(mesh):
    n_col, n_tm = mesh.shape["col"], mesh.shape["tm"]
    n_lane = 2 if n_col % 2 == 0 else 1
    dims = (n_col // n_lane, n_lane, n_tm)
    split = Mesh(mesh.devices.reshape(dims), ("grp", "lane", "tm"))
    col = ("grp", "lane")
    return jax.shard_map(
        functools.partial(body, dims),
        mesh=split,
        in_specs=(P(None, col), P("tm", col), P(None, "tm")),
        out_specs=(P(None, None, col), P()),
        check_vma=False,
    )
```

profile of v0, /device:TPU:0, one launch (start us, length us, event | category | flops | bytes accessed | tf_op | source)
XLA Modules:
  0.0 68.0 jit_solution(15055770628426381038)
XLA Ops:
  0.6 1.8 %shard_map.77 = s16[2,8,16,640]{3,2,1,0:T(8,128)(2,1)} custom-call(f32[32,600]{1,0:T(8,128)} %bitcast.20), custom_call_target="tpu_custom_call" | custom-call | tf_op jit(solution)/shard_map/pallas_call | solution.py:179
  2.5 8.4 %all-to-all-start = ((s16[16,16,640]{2,1,0:T(8,128)(2,1)}), s16[16,16,640]{2,1,0:T(8,128)(2,1)}, u32[]{:S(2)}, u32[]{:S(2)}) async-start(s16[16,16,640]{2,1,0:T(8,128)(2,1)} %bitcast.19), calls=%async_computation | async-start | bytes 655360 | tf_op jit(solution)/shard_map/all_to_all | solution.py:186
  10.8 1.9 %collective-permute-start = (s32[4,300]{1,0:T(4,128)}, s32[4,300]{1,0:T(4,128)S(1)}, u32[]{:S(2)}, u32[]{:S(2)}) collective-permute-start(s32[4,300]{1,0:T(4,128)} %param.8), channel_id=1, source_target_pairs={{0,1},{1,0},{2,3},{3,2},{4,5},{5,4},{6,7},{7,6},{8,9},{9,8},{10,11... | collective-permute-start | bytes 14408 | tf_op jit(solution)/shard_map/ppermute | solution.py:161
  12.7 0.0 copy-start.2
  12.7 1.9 %copy-done.2 = bf16[1280,1280]{1,0:T(8,128)(2,1)S(1)} copy-done((bf16[1280,1280]{1,0:T(8,128)(2,1)S(1)}, bf16[1280,1280]{1,0:T(8,128)(2,1)}, u32[]{:S(2)}) %copy-start.2) | copy-done | bytes 3276824
  14.7 0.0 copy-start.4
  14.7 1.9 %copy-done.4 = bf16[1280,1280]{1,0:T(8,128)(2,1)S(1)} copy-done((bf16[1280,1280]{1,0:T(8,128)(2,1)S(1)}, bf16[1280,1280]{1,0:T(8,128)(2,1)}, u32[]{:S(2)}) %copy-start.4) | copy-done | bytes 3276824
  16.6 0.0 copy-start.6
  16.6 2.0 %copy-done.6 = bf16[1200,1536]{1,0:T(8,128)(2,1)S(1)} copy-done((bf16[1200,1536]{1,0:T(8,128)(2,1)S(1)}, bf16[1200,1536]{1,0:T(8,128)(2,1)}, u32[]{:S(2)}) %copy-start.6) | copy-done | bytes 3686424
  18.6 0.0 copy-start.8
  18.6 0.0 copy-start.3
  18.6 0.0 copy-start.7
  18.6 14.3 %shard_map.78.cols_ref = bf16[1280,1536]{1,0:T(8,128)(2,1)S(1)} custom-call(bf16[1200,1536]{1,0:T(8,128)(2,1)S(1)} %copy-done.6, bf16[1280,1280]{1,0:T(8,128)(2,1)S(1)} %copy-done.2, bf16[1280,1280]{1,0:T(8,128)(2,1)S(1)} %copy-done.4), custom_call_target="tpu_custom_call" | custom-call | tf_op jit(solution)/shard_map/pallas_call | solution.py:196
  32.9 0.0 copy-start
  32.9 1.8 %copy-done = bf16[1280,1536]{1,0:T(8,128)(2,1)} copy-done((bf16[1280,1536]{1,0:T(8,128)(2,1)}, bf16[1280,1536]{1,0:T(8,128)(2,1)S(1)}, u32[]{:S(2)}) %copy-start) | copy-done | bytes 3932184
  34.8 0.0 collective-permute-done
  34.8 0.0 copy-done.8
  34.8 0.1 cosine_bitcast_fusion
  34.9 0.1 cos.11
  35.0 0.1 sin.11
  35.1 0.0 all-to-all-done
  35.1 0.0 collective-permute-start.1
  35.2 0.0 copy-done.3
  35.2 0.0 copy-done.7
  35.2 0.0 copy-start.1
  35.2 2.1 %copy-done.1 = bf16[1280,1536]{1,0:T(8,128)(2,1)S(1)} copy-done((bf16[1280,1536]{1,0:T(8,128)(2,1)S(1)}, bf16[1280,1536]{1,0:T(8,128)(2,1)}, u32[]{:S(2)}) %copy-start.1) | copy-done | bytes 3932184
  37.3 0.0 copy-start.5
  37.3 1.9 %copy-done.5 = bf16[1280,1280]{1,0:T(8,128)(2,1)S(1)} copy-done((bf16[1280,1280]{1,0:T(8,128)(2,1)S(1)}, bf16[1280,1280]{1,0:T(8,128)(2,1)}, u32[]{:S(2)}) %copy-start.5) | copy-done | bytes 3276824
  39.2 7.4 %shard_map.79 = f32[4,128]{1,0:T(4,128)S(1)} custom-call(s16[2,128,640]{2,1,0:T(8,128)(2,1)} %bitcast.2.code_ref, bf16[1280,1280]{1,0:T(8,128)(2,1)S(1)} %copy-done.3, bf16[1280,1280]{1,0:T(8,128)(2,1)S(1)} %copy-done.5, f32[2,1,1280]{2,1,0:T(1,128)S(1)} %copy-done.7, f32[8,640]{1,0:T(8,128)S(1)} %select_maximum_fusion.turn_ref, bf16[1280,1536]{1,0:T(8,128)(2,1)S(1)} %copy-done.1), custom_call_target="tpu_custom_call" | custom-call | tf_op jit(solution)/shard_map/pallas_call | solution.py:219
  46.6 0.0 collective-permute-done.1
  46.6 6.4 %shard_map.80 = f32[4,128]{1,0:T(4,128)S(1)} custom-call(s16[2,128,640]{2,1,0:T(8,128)(2,1)S(1)} %bitcast.18, bf16[1280,1280]{1,0:T(8,128)(2,1)S(1)} %copy-done.3, bf16[1280,1280]{1,0:T(8,128)(2,1)S(1)} %copy-done.5, f32[2,1,1280]{2,1,0:T(1,128)S(1)} %copy-done.7, f32[8,640]{1,0:T(8,128)S(1)} %select_maximum_fusion.turn_ref, bf16[1280,1536]{1,0:T(8,128)(2,1)S(1)} %copy-done.1), custom_call_target="tpu_custom_call" | custom-call | tf_op jit(solution)/shard_map/pallas_call | solution.py:219
  53.1 0.3 collective-permute-start.2
  53.3 0.6 broadcast_in_dim.15
  54.0 5.8 %all-to-all-start.1 = ((f32[32,4,128]{2,1,0:T(4,128)}), f32[32,4,128]{2,1,0:T(4,128)S(1)}, u32[]{:S(2)}, u32[]{:S(2)}) async-start(f32[32,4,128]{2,1,0:T(4,128)} %broadcast_in_dim.15), calls=%async_computation.1 | async-start | bytes 131072 | tf_op jit(solution)/shard_map/all_to_all | solution.py:224
  59.8 0.0 collective-permute-done.2
  59.8 0.1 stack.33
  59.9 0.1 stack.34
  60.0 0.1 copy.16
  60.0 0.7 %reshape.37 = f32[4,512,1]{1,2,0:T(1,128)} reshape(f32[4,8,2,2,16]{4,3,2,1,0:T(2,128)S(1)} %copy.16) | data formatting | bytes 16384 | tf_op jit(solution)/shard_map/reshape | solution.py:234
  60.8 6.6 %all-to-all-done.1 = f32[32,4,128]{2,1,0:T(4,128)S(1)} async-done(((f32[32,4,128]{2,1,0:T(4,128)}), f32[32,4,128]{2,1,0:T(4,128)S(1)}, u32[]{:S(2)}, u32[]{:S(2)}) %all-to-all-start.1) | async-done | bytes 65568 | tf_op jit(solution)/shard_map/all_to_all | solution.py:224
  67.4 0.7 reduce_max.9
  (10 shorter events, 0.1 us)
Async XLA Ops:
  2.5 32.6 %all-to-all-start = ((s16[16,16,640]{2,1,0:T(8,128)(2,1)}), s16[16,16,640]{2,1,0:T(8,128)(2,1)}, u32[]{:S(2)}, u32[]{:S(2)}) async-start(s16[16,16,640]{2,1,0:T(8,128)(2,1)} %bitcast.19), calls=%async_computation | async-start | bytes 655360 | tf_op jit(solution)/shard_map/all_to_all | solution.py:186
  10.8 23.9 %collective-permute-start = (s32[4,300]{1,0:T(4,128)}, s32[4,300]{1,0:T(4,128)S(1)}, u32[]{:S(2)}, u32[]{:S(2)}) collective-permute-start(s32[4,300]{1,0:T(4,128)} %param.8), channel_id=1, source_target_pairs={{0,1},{1,0},{2,3},{3,2},{4,5},{5,4},{6,7},{7,6},{8,9},{9,8},{10,11... | collective-permute-start | bytes 14408 | tf_op jit(solution)/shard_map/ppermute | solution.py:161
  12.7 1.9 %copy-start.2 = (bf16[1280,1280]{1,0:T(8,128)(2,1)S(1)}, bf16[1280,1280]{1,0:T(8,128)(2,1)}, u32[]{:S(2)}) copy-start(bf16[1280,1280]{1,0:T(8,128)(2,1)} %constant.31.clone.high_ref) | copy-start | bytes 9830404
  14.7 1.9 %copy-start.4 = (bf16[1280,1280]{1,0:T(8,128)(2,1)S(1)}, bf16[1280,1280]{1,0:T(8,128)(2,1)}, u32[]{:S(2)}) copy-start(bf16[1280,1280]{1,0:T(8,128)(2,1)} %constant.32.clone.low_ref) | copy-start | bytes 9830404
  16.6 2.0 %copy-start.6 = (bf16[1200,1536]{1,0:T(8,128)(2,1)S(1)}, bf16[1200,1536]{1,0:T(8,128)(2,1)}, u32[]{:S(2)}) copy-start(bf16[1200,1536]{1,0:T(8,128)(2,1)} %series_ref.1) | copy-start | bytes 11059204
  18.6 16.1 %copy-start.8 = (s32[4,300]{1,0:T(4,128)S(1)}, s32[4,300]{1,0:T(4,128)}, u32[]{:S(2)}) copy-start(s32[4,300]{1,0:T(4,128)} %param.8) | copy-start | bytes 14404
  18.6 16.5 %copy-start.3 = (bf16[1280,1280]{1,0:T(8,128)(2,1)S(1)}, bf16[1280,1280]{1,0:T(8,128)(2,1)}, u32[]{:S(2)}) copy-start(bf16[1280,1280]{1,0:T(8,128)(2,1)} %constant.31.clone.high_ref) | copy-start | bytes 9830404
  18.6 16.5 %copy-start.7 = (f32[2,1,1280]{2,1,0:T(1,128)S(1)}, f32[2,1,1280]{2,1,0:T(1,128)}, u32[]{:S(2)}) copy-start(f32[2,1,1280]{2,1,0:T(1,128)} %constant.33.clone.sums_ref) | copy-start | bytes 30724
  32.9 1.9 %copy-start = (bf16[1280,1536]{1,0:T(8,128)(2,1)}, bf16[1280,1536]{1,0:T(8,128)(2,1)S(1)}, u32[]{:S(2)}) copy-start(bf16[1280,1536]{1,0:T(8,128)(2,1)S(1)} %shard_map.78.cols_ref) | copy-start | bytes 11796484
  35.1 11.5 %collective-permute-start.1 = (s16[16,16,640]{2,1,0:T(8,128)(2,1)}, s16[16,16,640]{2,1,0:T(8,128)(2,1)S(1)}, u32[]{:S(2)}, u32[]{:S(2)}) collective-permute-start(s16[16,16,640]{2,1,0:T(8,128)(2,1)} %all-to-all-done), channel_id=1, source_target_pairs={{0,2},{2,0},{1,3},{3,1},{4,6},{6,4},{5,7},{7,5},{8,10},{10,8},{9,1... | collective-permute-start | bytes 983048 | tf_op jit(solution)/shard_map/ppermute | solution.py:209
  35.2 2.1 %copy-start.1 = (bf16[1280,1536]{1,0:T(8,128)(2,1)S(1)}, bf16[1280,1536]{1,0:T(8,128)(2,1)}, u32[]{:S(2)}) copy-start(bf16[1280,1536]{1,0:T(8,128)(2,1)} %copy-done) | copy-start | bytes 11796484
  37.3 1.9 %copy-start.5 = (bf16[1280,1280]{1,0:T(8,128)(2,1)S(1)}, bf16[1280,1280]{1,0:T(8,128)(2,1)}, u32[]{:S(2)}) copy-start(bf16[1280,1280]{1,0:T(8,128)(2,1)} %constant.32.clone.low_ref) | copy-start | bytes 9830404
  53.1 6.7 %collective-permute-start.2 = (f32[2,4,128]{2,1,0:T(4,128)S(1)}, f32[2,4,128]{2,1,0:T(4,128)S(1)}, u32[]{:S(2)}, u32[]{:S(2)}) collective-permute-start(f32[2,4,128]{2,1,0:T(4,128)S(1)} %pad_maximum_fusion), channel_id=1, source_target_pairs={{0,1},{1,0},{2,3},{3,2},{4,5},{5,4},{6,7},{7,6},{8,9},{9,8},{10,11... | collective-permute-start | bytes 12296 | tf_op jit(solution)/shard_map/ppermute | solution.py:161
  54.0 13.4 %all-to-all-start.1 = ((f32[32,4,128]{2,1,0:T(4,128)}), f32[32,4,128]{2,1,0:T(4,128)S(1)}, u32[]{:S(2)}, u32[]{:S(2)}) async-start(f32[32,4,128]{2,1,0:T(4,128)} %broadcast_in_dim.15), calls=%async_computation.1 | async-start | bytes 131072 | tf_op jit(solution)/shard_map/all_to_all | solution.py:224
where the time goes:
time: 68.6 us; the launch traced here: 68 us
  Pallas kernels  29.9 us (44%)
  starting transfers between devices  16.3 us (24%)
  local copies, waits for them, and re-layouts  13.6 us (20%)
  waiting for transfers between devices  6.62 us (10%)
  other arithmetic  0.83 us (1%)
  between operations  0.8 us (1%)
    pallas_call x1, Pallas kernels, body(): pl.pallas_call(functools.partial(column_kernel, share, share_pad), out_sh...  14.3 us
    pallas_call x2, Pallas kernels, body(): score(r.reshape(n_tm, rows, share_pad), high, low, sums, turn, cols)  13.8 us
    unnamed x18, local copies, waits for them, and re-layouts  11.8 us
    all_to_all x1, starting transfers between devices, body(): received = lax.all_to_all(codes, ('tm', 'grp'), 0, 0, tiled=True)  8.36 us
    all_to_all x1, waiting for transfers between devices, body(): lax.all_to_all(jnp.broadcast_to(best, (n_dev, surr, rows)), ('grp', 'lane...  6.61 us
    all_to_all x1, starting transfers between devices, body(): lax.all_to_all(jnp.broadcast_to(best, (n_dev, surr, rows)), ('grp', 'lane...  5.81 us
    ppermute x2, starting transfers between devices, tm_exchange(): other = lax.ppermute(value, 'tm', [(0, 1), (1, 0)])  2.15 us
    pallas_call x1, Pallas kernels, body(): pl.pallas_call(functools.partial(encode_kernel, share), out_shape=jax.Sha...  1.84 us
  transfers between devices with their start and end apart: 5, of which 1 were waited for; matrix products, arithmetic and copies ran while one was open for 3% of the time, Pallas kernels for 32%

commit v1 on v0

v1 whole, which is shorter than its diff:
```python
import functools
import math

import jax
import jax.numpy as jnp
import ml_dtypes
import numpy as np
from jax import lax
from jax.experimental import pallas as pl
from jax.experimental.pallas import tpu as pltpu
from jax.sharding import Mesh, PartitionSpec as P

EPSILON = 1e-06
LANES = 128
CODE_TOP = 32767.0
LOW_SCALE = 2.0**14
COARSE_SCALE = 2.0**6
COL_SCALE = 2.0**8
COL_REST_SCALE = LOW_SCALE * COL_SCALE / COARSE_SCALE
CODE_SCALE = COARSE_SCALE / LOW_SCALE
FLOAT8 = jnp.float8_e4m3fn
VMEM = pl.BlockSpec(memory_space=pltpu.VMEM)
HBM = pl.BlockSpec(memory_space=pltpu.HBM)
TILE = 2 * LANES


def round_up(value, unit):
    return -(-value // unit) * unit


def split_table(table, axis):
    high = table.astype(ml_dtypes.bfloat16)
    low = (table - high.astype(np.float64)) * LOW_SCALE
    low = np.concatenate([low, table * COARSE_SCALE], axis=axis).astype(ml_dtypes.float8_e4m3fn)
    return jnp.asarray(np.ascontiguousarray(high)), jnp.asarray(np.ascontiguousarray(low))


class Order:
    def __init__(self, freqs):
        self.half = round_up(-(-freqs // 2), 16)
        self.pad = round_up(2 * self.half, LANES)
        self.freq = np.zeros(self.pad, np.int64)
        self.freq[: freqs // 2] = np.arange(2, freqs + 1, 2)
        self.freq[self.half : self.half + freqs - freqs // 2] = np.arange(1, freqs + 1, 2)
        self.used = self.freq > 0

    def wave(self, points, frames):
        angles = (self.freq[:, None] * points[None, :] % frames) * (2.0 * math.pi / frames)
        return np.stack([np.cos(angles), np.sin(angles)]) * self.used[:, None]


def pad_last(array, size):
    return np.pad(array, [(0, 0)] * (array.ndim - 1) + [(0, size - array.shape[-1])])


def column_tables(frames, order):
    half_pad = round_up(frames // 2, LANES)
    wave = pad_last(order.wave(np.arange(frames // 2), frames), half_pad)[:, : 2 * order.half]
    wave = wave.reshape(2, 2, order.half, half_pad).transpose(1, 0, 2, 3)
    return split_table(wave.reshape(2, 2 * order.half, half_pad), 2)


def slab_tables(frames, share, n_tm, order):
    share_pad = round_up(share, LANES)
    wave = pad_last(order.wave(np.arange(share), frames), share_pad).transpose(0, 2, 1)
    high, low = split_table(wave, 1)
    sums = np.concatenate([wave[0].sum(axis=0), wave[1].sum(axis=0)])
    shift = order.wave(np.arange(n_tm) * share, frames).transpose(0, 2, 1)
    shift = np.concatenate([shift, shift], axis=2).reshape(2 * n_tm, 2 * order.pad)
    return high, low, jnp.asarray(np.concatenate([sums[None], shift]), jnp.float32)


def split_digits(value):
    scaled = value * 16.0
    first = scaled.astype(jnp.int32)
    rest = (scaled - first.astype(jnp.float32)) * 32768.0
    second = rest.astype(jnp.int32)
    third = ((rest - second.astype(jnp.float32)) * 32768.0).astype(jnp.int32)
    return first, second, third


def join_digits(first, second, third):
    return (
        first.astype(jnp.float32) * 2.0**-4
        + second.astype(jnp.float32) * 2.0**-19
        + third.astype(jnp.float32) * 2.0**-34
    )


def encode_kernel(share, slab_ref, code_ref):
    values = slab_ref[...]
    verts = values.shape[0]
    n_tm, n_grp, row_share, share_pad = code_ref.shape
    mean = jnp.sum(values, axis=1, keepdims=True) * (1.0 / share)
    offset = values - mean
    top = jnp.max(jnp.abs(offset), axis=1, keepdims=True)
    top_digits = split_digits(top)
    mean_digits = split_digits(mean)
    step = join_digits(*top_digits) * (1.0 / CODE_TOP)
    inverse = jnp.where(step > 0.0, 1.0 / jnp.where(step > 0.0, step, 1.0), 0.0)
    codes = jnp.clip(jnp.round(offset * inverse), -CODE_TOP, CODE_TOP).astype(jnp.int32)
    codes = jnp.concatenate(
        [codes, jnp.zeros((verts, share_pad - share), jnp.int32)], axis=1
    )
    lane = lax.broadcasted_iota(jnp.int32, (verts, share_pad), 1) - share
    for place, digit in enumerate(top_digits + mean_digits):
        codes = jnp.where(lane == place, digit, codes)
    for m in range(n_tm):
        block = codes[m * row_share : (m + 1) * row_share].astype(jnp.int16)
        for g in range(n_grp):
            code_ref[m, g] = block


def start_copy(source, target, sem):
    copy = pltpu.make_async_copy(source, target, sem)
    copy.start()
    return copy


def wait_all(copies):
    for copy in copies:
        copy.wait()


def column_kernel(
    series_hbm, high_hbm, low_hbm, out_hbm,
    series, high, low, out, normed_0, normed_1, coarse_0, coarse_1, load_sems, store_sems,
):
    n_tiles, frames, _ = series.shape
    half = frames // 2
    half_pad = high.shape[2]
    freq_half = high.shape[1] // 2
    freq_pad = out.shape[1] // 2
    gap = freq_pad - 2 * freq_half
    normed_refs, coarse_refs = (normed_0, normed_1), (coarse_0, coarse_1)

    def load_tile(j):
        return start_copy(series_hbm.at[:, pl.ds(j * TILE, TILE)], series.at[j], load_sems.at[j])

    tile_copies = [load_tile(0)]
    table_copies = [
        start_copy(high_hbm, high, load_sems.at[n_tiles]),
        start_copy(low_hbm, low, load_sems.at[n_tiles + 1]),
    ]
    tile_copies += [load_tile(j) for j in range(1, n_tiles)]

    def normalize(j):
        normed_ref, coarse_ref = normed_refs[j % 2], coarse_refs[j % 2]
        values = series[j].astype(jnp.float32)
        centered = values - jnp.sum(values, axis=0, keepdims=True) * (1.0 / frames)
        total = jnp.sum(centered * centered, axis=0, keepdims=True)
        normed = (centered * lax.rsqrt(total + EPSILON)).astype(jnp.bfloat16).astype(jnp.float32)
        first, second = normed[:half], normed[half:]
        for parity, part in enumerate((first + second, first - second)):
            if half_pad > half:
                part = jnp.concatenate([part, jnp.zeros((half_pad - half, TILE), jnp.float32)], axis=0)
            rounded = part.astype(jnp.bfloat16)
            rest = part - rounded.astype(jnp.float32)
            normed_ref[parity] = rounded
            coarse_ref[parity, pl.ds(0, half_pad), :] = (part * COL_SCALE).astype(FLOAT8)
            coarse_ref[parity, pl.ds(half_pad, half_pad), :] = (rest * COL_REST_SCALE).astype(FLOAT8)

    tile_copies[0].wait()
    normalize(0)
    wait_all(table_copies + tile_copies[1:2])
    stores = []
    for j in range(n_tiles):
        if j == 1:
            wait_all(tile_copies[2:])
        if j + 1 < n_tiles:
            normalize(j + 1)
        for parity in range(2):
            sums = jnp.dot(
                high[parity], normed_refs[j % 2][parity], preferred_element_type=jnp.float32
            )
            rest = jnp.dot(
                low[parity], coarse_refs[j % 2][parity], preferred_element_type=jnp.float32
            )
            sums = (sums + rest * (1.0 / (LOW_SCALE * COL_SCALE))).astype(jnp.bfloat16)
            for q in range(2):
                span = pl.ds(q * freq_pad + parity * freq_half, freq_half)
                out[j, span, :] = sums[q * freq_half : (q + 1) * freq_half]
        for q in range(2):
            if gap:
                span = pl.ds(q * freq_pad + 2 * freq_half, gap)
                out[j, span, :] = jnp.zeros((gap, TILE), jnp.bfloat16)
        stores.append(start_copy(out.at[j], out_hbm.at[j], store_sems.at[j]))
    wait_all(stores)


def spectrum_kernel(
    share, codes_hbm, high_hbm, low_hbm, cols_hbm, shift_ref, spec_ref, cols_ref,
    codes_ref, high, low, sems,
):
    n_tm, rows, share_pad = codes_ref.shape
    freq_pad = high.shape[2]
    codes_copy = start_copy(codes_hbm, codes_ref, sems.at[0])
    copies = [
        [
            start_copy(high_hbm.at[q], high.at[q], sems.at[1 + 2 * q]),
            start_copy(low_hbm.at[q], low.at[q], sems.at[2 + 2 * q]),
        ]
        for q in range(2)
    ]
    cols_copy = start_copy(cols_hbm.at[pl.ds(0, cols_ref.shape[0])], cols_ref, sems.at[5])
    codes_copy.wait()
    codes = codes_ref[...].reshape(n_tm * rows, share_pad).astype(jnp.int32)
    upper = ((codes + 128) >> 8) << 8
    lower = (codes - upper).astype(jnp.float32)
    upper = upper.astype(jnp.float32)
    coarse = jnp.concatenate([upper * CODE_SCALE, lower], axis=1).astype(FLOAT8)
    upper = upper.astype(jnp.bfloat16)
    digits = [codes[:, share + p : share + p + 1] for p in range(6)]
    step = join_digits(*digits[:3]) * (1.0 / CODE_TOP)
    mean = join_digits(*digits[3:])
    parts = []
    for q in range(2):
        wait_all(copies[q])
        part = jnp.dot(upper, high[q], preferred_element_type=jnp.float32)
        part += jnp.dot(coarse, low[q], preferred_element_type=jnp.float32) * (1.0 / COARSE_SCALE)
        part = part * step + mean * shift_ref[0:1, q * freq_pad : (q + 1) * freq_pad]
        if n_tm == 2:
            sign = shift_ref[2:3, :freq_pad]
            spec_ref[:, q * freq_pad : (q + 1) * freq_pad] = part[:rows] + part[rows:] * sign
        parts.append(part)
    if n_tm != 2:
        spec_cos = jnp.zeros((rows, freq_pad), jnp.float32)
        spec_sin = jnp.zeros((rows, freq_pad), jnp.float32)
        for m in range(n_tm):
            part_cos, part_sin = (part[m * rows : (m + 1) * rows] for part in parts)
            shift_cos = shift_ref[1 + m : 2 + m, :freq_pad]
            shift_sin = shift_ref[1 + n_tm + m : 2 + n_tm + m, :freq_pad]
            spec_cos += part_cos * shift_cos - part_sin * shift_sin
            spec_sin += part_sin * shift_cos + part_cos * shift_sin
        spec_ref[:, :freq_pad] = spec_cos
        spec_ref[:, freq_pad:] = spec_sin
    cols_copy.wait()


def rotate(frames, last_freq, spec_ref, turn_ref, rot_ref):
    rows = spec_ref.shape[0]
    surr, freq_pad = turn_ref.shape[0] // 2, turn_ref.shape[1]
    spec_cos = spec_ref[:, :freq_pad]
    spec_sin = spec_ref[:, freq_pad:]
    freq = lax.broadcasted_iota(jnp.int32, (1, freq_pad), 1)
    pair = jnp.where(freq != last_freq, (2.0 / frames) ** 2 * (frames / 2.0), 0.0)
    last = jnp.where(freq == last_freq, float(frames), 0.0)
    common = jnp.sum((spec_cos * spec_cos + spec_sin * spec_sin) * pair, axis=1, keepdims=True)
    scales = []
    for s in range(surr):
        cos_row = turn_ref[pl.ds(s, 1), :]
        sin_row = turn_ref[pl.ds(surr + s, 1), :]
        rot_real = spec_cos * cos_row + spec_sin * sin_row
        rot_imag = spec_cos * sin_row - spec_sin * cos_row
        energy = common + jnp.sum(rot_real * rot_real * last, axis=1, keepdims=True)
        scales.append(lax.rsqrt(energy + EPSILON) * math.sqrt(frames))
        span = pl.ds(s * rows, rows)
        rot_ref[span, :freq_pad] = rot_real.astype(jnp.bfloat16)
        rot_ref[span, freq_pad:] = (-rot_imag).astype(jnp.bfloat16)
    return scales


def raise_top(top, rot, cols_ref):
    for j in range(cols_ref.shape[0]):
        scores = jnp.abs(jnp.dot(rot, cols_ref[j], preferred_element_type=jnp.float32))
        for part in range(0, TILE, LANES):
            top = jnp.maximum(top, scores[:, part : part + LANES])
    return top


def row_peaks(top, scales):
    rows = scales[0].shape[0]
    peaks = [
        jnp.max((top[s * rows : (s + 1) * rows] * scale).T, axis=0, keepdims=True)
        for s, scale in enumerate(scales)
    ]
    return jnp.concatenate(peaks, axis=0)


def first_score_kernel(
    frames, last_freq, spec_ref, turn_ref, near_ref, cols_hbm, peak_ref, far_ref, rot_ref, sem
):
    n_near = near_ref.shape[0]
    copy = start_copy(cols_hbm.at[pl.ds(n_near, far_ref.shape[0])], far_ref, sem)
    scales = rotate(frames, last_freq, spec_ref, turn_ref, rot_ref)
    rot = rot_ref[...]
    top = raise_top(jnp.zeros((rot.shape[0], LANES), jnp.float32), rot, near_ref)
    copy.wait()
    peak_ref[...] = row_peaks(raise_top(top, rot, far_ref), scales)


def second_score_kernel(
    frames, last_freq, spec_ref, turn_ref, near_ref, far_ref, first_ref, own_ref, best_ref, rot_ref
):
    scales = rotate(frames, last_freq, spec_ref, turn_ref, rot_ref)
    rot = rot_ref[...]
    top = raise_top(jnp.zeros((rot.shape[0], LANES), jnp.float32), rot, near_ref)
    peaks = row_peaks(raise_top(top, rot, far_ref), scales)
    first = first_ref[...]
    own_ref[0] = first
    own_ref[1] = peaks
    best_ref[...] = jnp.broadcast_to(jnp.maximum(first, peaks)[None], best_ref.shape)


def tm_exchange(value, n_tm):
    if n_tm == 2:
        other = lax.ppermute(value, "tm", [(0, 1), (1, 0)])
        first = lax.axis_index("tm") == 0
        return jnp.stack([jnp.where(first, value, other), jnp.where(first, other, value)])
    return lax.all_gather(value, "tm")


def in_hbm(array):
    return pltpu.with_memory_space_constraint(array, pltpu.HBM)


def body(dims, series, slab_series, phase_index):
    n_grp, n_lane, n_tm = dims
    frames, columns = series.shape
    share, verts = slab_series.shape
    surr = phase_index.shape[0]
    freqs = phase_index.shape[1] * n_tm
    row_share = verts // n_tm
    rows = n_grp * row_share
    share_pad = round_up(share, LANES)
    half_pad = round_up(frames // 2, LANES)
    order = Order(freqs)
    last_freq = int(np.argmax(order.freq))
    points = 2 * order.pad
    limits = pltpu.CompilerParams(vmem_limit_bytes=24 * 2**20)

    codes = pl.pallas_call(
        functools.partial(encode_kernel, share),
        out_shape=jax.ShapeDtypeStruct((n_tm, n_grp, row_share, share_pad), jnp.int16),
        in_specs=[VMEM],
        out_specs=VMEM,
    )(slab_series.T)
    codes = codes.reshape(n_tm * n_grp, row_share, share_pad)
    received = lax.all_to_all(codes, ("tm", "grp"), 0, 0, tiled=True)

    phase = tm_exchange(phase_index, n_tm)
    phase = jnp.transpose(phase, (1, 0, 2)).reshape(surr, freqs)
    angle = phase.astype(jnp.float32) * (2.0 * math.pi / frames)
    weight = jnp.where(jnp.arange(1, freqs + 1) < freqs, 2.0, 1.0) / frames
    turn = jnp.concatenate([jnp.cos(angle) * weight, jnp.sin(angle) * weight], axis=0)
    gap = jnp.zeros((2 * surr, order.half - freqs // 2), jnp.float32)
    turn = jnp.concatenate([turn[:, 1::2], gap, turn[:, 0::2]], axis=1)
    turn = jnp.pad(turn, ((0, 0), (0, order.pad - turn.shape[1])))

    n_tiles = columns // TILE
    col_high, col_low = column_tables(frames, order)
    cols = pl.pallas_call(
        column_kernel,
        out_shape=pltpu.HBM((n_tiles, points, TILE), jnp.bfloat16),
        in_specs=[HBM] * 3,
        out_specs=HBM,
        scratch_shapes=[
            pltpu.VMEM((n_tiles, frames, TILE), jnp.bfloat16),
            pltpu.VMEM(col_high.shape, jnp.bfloat16),
            pltpu.VMEM(col_low.shape, FLOAT8),
            pltpu.VMEM((n_tiles, points, TILE), jnp.bfloat16),
        ]
        + [pltpu.VMEM((2, half_pad, TILE), jnp.bfloat16)] * 2
        + [pltpu.VMEM((2, 2 * half_pad, TILE), FLOAT8)] * 2
        + [pltpu.SemaphoreType.DMA((n_tiles + 2,)), pltpu.SemaphoreType.DMA((n_tiles,))],
        compiler_params=limits,
        cost_estimate=pl.CostEstimate(
            flops=6 * order.pad * frames * columns, transcendentals=0, bytes_accessed=0
        ),
    )(in_hbm(series), in_hbm(col_high), in_hbm(col_low))

    received, cols, turn = lax.optimization_barrier((received, cols, turn))
    high, low, shift = slab_tables(frames, share, n_tm, order)
    n_near = n_tiles // 2
    spec, near = pl.pallas_call(
        functools.partial(spectrum_kernel, share),
        out_shape=(
            jax.ShapeDtypeStruct((rows, points), jnp.float32),
            pltpu.VMEM((n_near, points, TILE), jnp.bfloat16),
        ),
        in_specs=[HBM] * 4 + [VMEM],
        out_specs=(VMEM, VMEM),
        scratch_shapes=[
            pltpu.VMEM((n_tm, rows, share_pad), jnp.int16),
            pltpu.VMEM(high.shape, jnp.bfloat16),
            pltpu.VMEM(low.shape, FLOAT8),
            pltpu.SemaphoreType.DMA((6,)),
        ],
        compiler_params=limits,
        cost_estimate=pl.CostEstimate(
            flops=4 * points * n_tm * share_pad * rows, transcendentals=0, bytes_accessed=0
        ),
    )(
        in_hbm(received.reshape(n_tm, rows, share_pad)),
        in_hbm(high), in_hbm(low), in_hbm(cols), shift,
    )
    other = lax.ppermute(spec, "lane", [(i, (i + 1) % n_lane) for i in range(n_lane)])
    score_cost = pl.CostEstimate(
        flops=2 * points * surr * rows * columns, transcendentals=0, bytes_accessed=0
    )
    rot_shape = pltpu.VMEM((surr * rows, points), jnp.bfloat16)
    first, far = pl.pallas_call(
        functools.partial(first_score_kernel, frames, last_freq),
        out_shape=(
            jax.ShapeDtypeStruct((surr, rows), jnp.float32),
            pltpu.VMEM((n_tiles - n_near, points, TILE), jnp.bfloat16),
        ),
        in_specs=[VMEM] * 3 + [HBM],
        out_specs=(VMEM, VMEM),
        scratch_shapes=[rot_shape, pltpu.SemaphoreType.DMA],
        compiler_params=limits,
        cost_estimate=score_cost,
    )(spec, turn, near, in_hbm(cols))
    n_dev = n_grp * n_lane * n_tm
    own, best = pl.pallas_call(
        functools.partial(second_score_kernel, frames, last_freq),
        out_shape=(
            jax.ShapeDtypeStruct((2, surr, rows), jnp.float32),
            jax.ShapeDtypeStruct((n_dev, surr, rows), jnp.float32),
        ),
        in_specs=[VMEM] * 5,
        out_specs=(VMEM, VMEM),
        scratch_shapes=[rot_shape],
        compiler_params=limits,
        cost_estimate=score_cost,
    )(other, turn, near, far, first)
    every = lax.all_to_all(best, ("grp", "lane", "tm"), 0, 0, tiled=True)
    peak_all = jnp.max(every, axis=(0, 2))

    own = jnp.where(lax.axis_index("lane") == 0, own, own[::-1])[:n_lane]
    both = tm_exchange(own, n_tm).reshape(n_tm, n_lane, surr, n_grp, row_share)
    tile_peak = jnp.transpose(both, (2, 3, 1, 0, 4)).reshape(surr, -1, 1)
    return tile_peak, peak_all


def solution(mesh):
    n_col, n_tm = mesh.shape["col"], mesh.shape["tm"]
    n_lane = 2 if n_col % 2 == 0 else 1
    dims = (n_col // n_lane, n_lane, n_tm)
    split = Mesh(mesh.devices.reshape(dims), ("grp", "lane", "tm"))
    col = ("grp", "lane")
    return jax.shard_map(
        functools.partial(body, dims),
        mesh=split,
        in_specs=(P(None, col), P("tm", col), P(None, "tm")),
        out_specs=(P(None, None, col), P()),
        check_vma=False,
    )
```

time: 68.6 us -> 48.3 us (0.70)
  local copies, waits for them, and re-layouts: 13.6 us -> 2.71 us
  Pallas kernels: 29.9 us -> 21.4 us
  starting transfers between devices: 16.3 us -> 15.5 us
    unnamed x18 -> x6, local copies, waits for them, and re-layouts: 11.8 us -> 0.72 us
    pallas_call x3 -> x4, Pallas kernels: 28.1 us -> 19.6 us  [the longest x1 10.3 us: body(): pl.pallas_call(column_kernel, out_shape=pltpu.HBM((n_tiles, points, TILE)...]
    ppermute x2, starting transfers between devices: 2.15 us -> 4.96 us  [tm_exchange(): other = lax.ppermute(value, 'tm', [(0, 1), (1, 0)])]
    all_to_all x1, starting transfers between devices: 8.36 us -> 5.91 us  [body(): received = lax.all_to_all(codes, ('tm', 'grp'), 0, 0, tiled=True)]
    all_to_all x1, starting transfers between devices: 5.81 us -> 4.52 us  [body(): every = lax.all_to_all(best, ('grp', 'lane', 'tm'), 0, 0, tiled=True)]
    slice x0 -> x2, local copies, waits for them, and re-layouts: none -> 0.77 us  [body(): turn = jnp.concatenate([turn[:, 1::2], gap, turn[:, 0::2]], axis=1)]
  transfers between devices with their start and end apart: 5 -> 5, of which waited for: 1 -> 1; matrix products, arithmetic and copies ran while one was open for 3% -> 5% of each run, Pallas kernels for 32% -> 32%
where the time goes in v1:
time: 48.3 us; the launch traced here: 47.9 us
  Pallas kernels  21.4 us (44%)
  starting transfers between devices  15.5 us (32%)
  waiting for transfers between devices  6.62 us (14%)
  local copies, waits for them, and re-layouts  2.71 us (6%)
  other arithmetic  0.89 us (2%)
  between operations  0.81 us (2%)
    pallas_call x1, Pallas kernels, body(): pl.pallas_call(column_kernel, out_shape=pltpu.HBM((n_tiles, points, TILE)...  10.3 us
    all_to_all x1, waiting for transfers between devices, body(): every = lax.all_to_all(best, ('grp', 'lane', 'tm'), 0, 0, tiled=True)  6.61 us
    all_to_all x1, starting transfers between devices, body(): received = lax.all_to_all(codes, ('tm', 'grp'), 0, 0, tiled=True)  5.91 us
    ppermute x2, starting transfers between devices, tm_exchange(): other = lax.ppermute(value, 'tm', [(0, 1), (1, 0)])  4.96 us
    all_to_all x1, starting transfers between devices, body(): every = lax.all_to_all(best, ('grp', 'lane', 'tm'), 0, 0, tiled=True)  4.52 us
    pallas_call x1, Pallas kernels, body(): pl.pallas_call(functools.partial(first_score_kernel, frames, last_freq),...  3.37 us
    pallas_call x1, Pallas kernels, body(): pl.pallas_call(functools.partial(second_score_kernel, frames, last_freq),...  3 us
    pallas_call x1, Pallas kernels, body(): pl.pallas_call(functools.partial(spectrum_kernel, share), out_shape=(jax....  3 us
  transfers between devices with their start and end apart: 5, of which 1 were waited for; matrix products, arithmetic and copies ran while one was open for 5% of the time, Pallas kernels for 32%

profile of v1, /device:TPU:0, one launch (start us, length us, event | category | flops | bytes accessed | tf_op | source)
XLA Modules:
  0.0 47.9 jit_solution(16989658332665572301)
XLA Ops:
  0.6 3.0 %collective-permute-start = (s32[4,300]{1,0:T(4,128)}, s32[4,300]{1,0:T(4,128)S(1)}, u32[]{:S(2)}, u32[]{:S(2)}) collective-permute-start(s32[4,300]{1,0:T(4,128)} %param.10), channel_id=1, source_target_pairs={{0,1},{1,0},{2,3},{3,2},{4,5},{5,4},{6,7},{7,6},{8,9},{9,8},{10,11... | collective-permute-start | bytes 14408 | tf_op jit(solution)/shard_map/ppermute | solution.py:307
  3.7 1.8 %shard_map.95 = s16[2,8,16,640]{3,2,1,0:T(8,128)(2,1)} custom-call(f32[32,600]{1,0:T(8,128)} %bitcast.15), custom_call_target="tpu_custom_call" | custom-call | tf_op jit(solution)/shard_map/pallas_call | solution.py:332
  5.5 5.9 %all-to-all-start = ((s16[16,16,640]{2,1,0:T(8,128)(2,1)}), s16[16,16,640]{2,1,0:T(8,128)(2,1)S(1)}, u32[]{:S(2)}, u32[]{:S(2)}) async-start(s16[16,16,640]{2,1,0:T(8,128)(2,1)} %bitcast.14), calls=%async_computation | async-start | bytes 655360 | tf_op jit(solution)/shard_map/all_to_all | solution.py:339
  11.4 0.0 copy-start.2
  11.4 0.0 copy-start
  11.4 10.3 %shard_map.96.cols_hbm = bf16[6,1280,256]{2,1,0:T(8,128)(2,1)} custom-call(bf16[1200,1536]{1,0:T(8,128)(2,1)} %series_hbm.1, bf16[2,608,640]{2,1,0:T(8,128)(2,1)} %constant.36.clone.high_hbm, f8e4m3fn[2,608,1280]{2,1,0:T(32,128)(4,1)} %constant.37.clone.low_hbm), custom_call_target="tpu_custom_call" | custom-call | flops 7077888000 | tf_op jit(solution)/shard_map/pallas_call | solution.py:352
  21.7 0.1 pad.8.clone
  21.8 0.0 collective-permute-done
  21.8 0.0 copy-done.2
  21.8 0.1 cosine_bitcast_fusion
  21.9 0.1 cos.11
  22.0 0.1 sin.11
  22.1 0.4 slice.7
  22.5 0.4 slice.6
  22.9 0.1 pad_maximum_fusion.1
  23.0 0.0 all-to-all-done
  23.0 0.0 copy-start.1
  23.0 0.7 %copy-done.1 = s16[16,16,640]{2,1,0:T(8,128)(2,1)} copy-done((s16[16,16,640]{2,1,0:T(8,128)(2,1)}, s16[16,16,640]{2,1,0:T(8,128)(2,1)S(1)}, u32[]{:S(2)}) %copy-start.1) | copy-done | bytes 327704
  23.7 0.0 copy-done
  23.7 3.0 %shard_map.97 = (f32[128,1280]{1,0:T(8,128)S(1)}, bf16[3,1280,256]{2,1,0:T(8,128)(2,1)S(1)}) custom-call(s16[2,128,640]{2,1,0:T(8,128)(2,1)} %bitcast.13, bf16[2,640,640]{2,1,0:T(8,128)(2,1)} %constant.38.clone.high_hbm, f8e4m3fn[2,1280,640]{2,1,0:T(32,128)(4,1)} %constant.39.clone.low_hbm, bf16[6,1280,256]{2,1,0:T(8,128)(2,1)} %shard_map.96.cols_hbm, ...), custom_call_target="tpu_custom_call" | custom-call | flops 838860800 | tf_op jit(solution)/shard_map/pallas_call | solution.py:375
  26.7 0.1 collective-permute-start.1
  26.8 3.4 %shard_map.98 = (f32[4,128]{1,0:T(4,128)S(1)}, bf16[3,1280,256]{2,1,0:T(8,128)(2,1)S(1)}) custom-call(f32[128,1280]{1,0:T(8,128)S(1)} %get-tuple-element.13.spec_ref, f32[8,640]{1,0:T(8,128)S(1)} %pad.4.turn_ref, bf16[3,1280,256]{2,1,0:T(8,128)(2,1)S(1)} %get-tuple-element.15.near_ref, bf16[6,1280,256]{2,1,0:T(8,128)(2,1)} %shard_map.96.cols_hbm), custom_call_target="tpu_custom_call" | custom-call | flops 2013265920 | tf_op jit(solution)/shard_map/pallas_call | solution.py:402
  30.2 0.0 collective-permute-done.1.spec_ref
  30.2 3.0 %shard_map.99 = (f32[2,4,128]{2,1,0:T(4,128)S(1)}, f32[32,4,128]{2,1,0:T(4,128)}) custom-call(f32[128,1280]{1,0:T(8,128)S(1)} %collective-permute-done.1.spec_ref, f32[8,640]{1,0:T(8,128)S(1)} %pad.4.turn_ref, bf16[3,1280,256]{2,1,0:T(8,128)(2,1)S(1)} %get-tuple-element.15.near_ref, bf16[3,1280,256]{2,1,0:T(8,128)(2,1)S(1)} %get-tuple-element.16.far_ref, ...), custom_call_target="tpu_custom_call" | custom-call | flops 2013265920 | tf_op jit(solution)/shard_map/pallas_call | solution.py:415
  33.2 1.9 %collective-permute-start.2 = (f32[2,4,128]{2,1,0:T(4,128)S(1)}, f32[2,4,128]{2,1,0:T(4,128)S(1)}, u32[]{:S(2)}, u32[]{:S(2)}) collective-permute-start(f32[2,4,128]{2,1,0:T(4,128)S(1)} %reverse_select_fusion), channel_id=1, source_target_pairs={{0,1},{1,0},{2,3},{3,2},{4,5},{5,4},{6,7},{7,6},{8,9},{9,8},{10,11... | collective-permute-start | bytes 12296 | tf_op jit(solution)/shard_map/ppermute | solution.py:307
  35.1 4.5 %all-to-all-start.1 = ((f32[32,4,128]{2,1,0:T(4,128)}), f32[32,4,128]{2,1,0:T(4,128)S(1)}, u32[]{:S(2)}, u32[]{:S(2)}) async-start(f32[32,4,128]{2,1,0:T(4,128)} %get-tuple-element.19), calls=%async_computation.1 | async-start | bytes 131072 | tf_op jit(solution)/shard_map/all_to_all | solution.py:427
  39.7 0.0 collective-permute-done.2
  39.7 0.1 stack.21
  39.8 0.1 stack.22
  39.9 0.1 copy.12
  39.9 0.7 %reshape.33 = f32[4,512,1]{1,2,0:T(1,128)} reshape(f32[4,8,2,2,16]{4,3,2,1,0:T(2,128)S(1)} %copy.12) | data formatting | bytes 16384 | tf_op jit(solution)/shard_map/reshape | solution.py:432
  40.7 6.6 %all-to-all-done.1 = f32[32,4,128]{2,1,0:T(4,128)S(1)} async-done(((f32[32,4,128]{2,1,0:T(4,128)}), f32[32,4,128]{2,1,0:T(4,128)S(1)}, u32[]{:S(2)}, u32[]{:S(2)}) %all-to-all-start.1) | async-done | bytes 65568 | tf_op jit(solution)/shard_map/all_to_all | solution.py:427
  47.3 0.7 %reduce_max.9 = f32[4]{0:T(128)} reduce(f32[32,4,128]{2,1,0:T(4,128)S(1)} %all-to-all-done.1, f32[]{:T(128)} %constant.35.clone.1), dimensions={0,2}, to_apply=%region_0.1 | reduce | flops 16380 | bytes 65556 | tf_op jit(solution)/shard_map/reduce_max | solution.py:428
  (11 shorter events, 0.1 us)
Async XLA Ops:
  0.6 21.2 %collective-permute-start = (s32[4,300]{1,0:T(4,128)}, s32[4,300]{1,0:T(4,128)S(1)}, u32[]{:S(2)}, u32[]{:S(2)}) collective-permute-start(s32[4,300]{1,0:T(4,128)} %param.10), channel_id=1, source_target_pairs={{0,1},{1,0},{2,3},{3,2},{4,5},{5,4},{6,7},{7,6},{8,9},{9,8},{10,11... | collective-permute-start | bytes 14408 | tf_op jit(solution)/shard_map/ppermute | solution.py:307
  5.5 17.5 %all-to-all-start = ((s16[16,16,640]{2,1,0:T(8,128)(2,1)}), s16[16,16,640]{2,1,0:T(8,128)(2,1)S(1)}, u32[]{:S(2)}, u32[]{:S(2)}) async-start(s16[16,16,640]{2,1,0:T(8,128)(2,1)} %bitcast.14), calls=%async_computation | async-start | bytes 655360 | tf_op jit(solution)/shard_map/all_to_all | solution.py:339
  11.4 10.4 %copy-start.2 = (s32[4,300]{1,0:T(4,128)S(1)}, s32[4,300]{1,0:T(4,128)}, u32[]{:S(2)}) copy-start(s32[4,300]{1,0:T(4,128)} %param.10) | copy-start | bytes 14404
  11.4 12.3 %copy-start = (f32[5,1280]{1,0:T(8,128)S(1)}, f32[5,1280]{1,0:T(8,128)}, u32[]{:S(2)}) copy-start(f32[5,1280]{1,0:T(8,128)} %constant.40.clone.shift_ref) | copy-start | bytes 76804
  23.0 0.7 %copy-start.1 = (s16[16,16,640]{2,1,0:T(8,128)(2,1)}, s16[16,16,640]{2,1,0:T(8,128)(2,1)S(1)}, u32[]{:S(2)}) copy-start(s16[16,16,640]{2,1,0:T(8,128)(2,1)S(1)} %all-to-all-done) | copy-start | bytes 983044
  26.7 3.5 %collective-permute-start.1 = (f32[128,1280]{1,0:T(8,128)S(1)}, f32[128,1280]{1,0:T(8,128)S(1)}, u32[]{:S(2)}, u32[]{:S(2)}) collective-permute-start(f32[128,1280]{1,0:T(8,128)S(1)} %get-tuple-element.13.spec_ref), channel_id=1, source_target_pairs={{0,2},{2,0},{1,3},{3,1},{4,6},{6,4},{5,7},{7,5},{8,10},{10,8},{9,1... | collective-permute-start | bytes 1966088 | tf_op jit(solution)/shard_map/ppermute | solution.py:397
  33.2 6.5 %collective-permute-start.2 = (f32[2,4,128]{2,1,0:T(4,128)S(1)}, f32[2,4,128]{2,1,0:T(4,128)S(1)}, u32[]{:S(2)}, u32[]{:S(2)}) collective-permute-start(f32[2,4,128]{2,1,0:T(4,128)S(1)} %reverse_select_fusion), channel_id=1, source_target_pairs={{0,1},{1,0},{2,3},{3,2},{4,5},{5,4},{6,7},{7,6},{8,9},{9,8},{10,11... | collective-permute-start | bytes 12296 | tf_op jit(solution)/shard_map/ppermute | solution.py:307
  35.1 12.1 %all-to-all-start.1 = ((f32[32,4,128]{2,1,0:T(4,128)}), f32[32,4,128]{2,1,0:T(4,128)S(1)}, u32[]{:S(2)}, u32[]{:S(2)}) async-start(f32[32,4,128]{2,1,0:T(4,128)} %get-tuple-element.19), calls=%async_computation.1 | async-start | bytes 131072 | tf_op jit(solution)/shard_map/all_to_all | solution.py:427

commit v2 on v1

--- a/solution.py
+++ b/solution.py
@@ -60,14 +60,23 @@
     return split_table(wave.reshape(2, 2 * order.half, half_pad), 2)
 
 
-def slab_tables(frames, share, n_tm, order):
-    share_pad = round_up(share, LANES)
+def slab_tables(frames, share, share_pad, n_tm, order):
     wave = pad_last(order.wave(np.arange(share), frames), share_pad).transpose(0, 2, 1)
     high, low = split_table(wave, 1)
     sums = np.concatenate([wave[0].sum(axis=0), wave[1].sum(axis=0)])
     shift = order.wave(np.arange(n_tm) * share, frames).transpose(0, 2, 1)
     shift = np.concatenate([shift, shift], axis=2).reshape(2 * n_tm, 2 * order.pad)
     return high, low, jnp.asarray(np.concatenate([sums[None], shift]), jnp.float32)
+
+
+def placement(order, freqs, n_tm, rows):
+    share = freqs // n_tm
+    share_pad = round_up(share, rows)
+    index = order.freq - 1
+    row = index // share * share_pad + index % share
+    table = np.zeros((n_tm * share_pad, order.pad), ml_dtypes.float8_e4m3fn)
+    table[row[order.used], np.nonzero(order.used)[0]] = 1.0
+    return jnp.asarray(table)
 
 
 def split_digits(value):
@@ -87,7 +96,15 @@
     )
 
 
-def encode_kernel(share, slab_ref, code_ref):
+def phase_lane(share):
+    return round_up(share + 6, 8)
+
+
+def phase_chunks(freq_share, rows):
+    return -(-freq_share // rows)
+
+
+def encode_kernel(share, rows, slab_ref, phase_ref, code_ref):
     values = slab_ref[...]
     verts = values.shape[0]
     n_tm, n_grp, row_share, share_pad = code_ref.shape
@@ -105,6 +122,27 @@
     lane = lax.broadcasted_iota(jnp.int32, (verts, share_pad), 1) - share
     for place, digit in enumerate(top_digits + mean_digits):
         codes = jnp.where(lane == place, digit, codes)
+
+    surr, freq_share = phase_ref.shape
+    chunks = phase_chunks(freq_share, rows)
+    phase = phase_ref[...].astype(jnp.float32)
+    phase = jnp.concatenate(
+        [phase, jnp.zeros((surr, chunks * rows - freq_share), jnp.float32)], axis=1
+    )
+    phase = jnp.concatenate([phase[:, c * rows : (c + 1) * rows] for c in range(chunks)], axis=0)
+    above = phase_lane(share) % LANES
+    phase = jnp.concatenate(
+        [
+            jnp.zeros((above, rows), jnp.float32),
+            phase,
+            jnp.zeros((LANES - above - chunks * surr, rows), jnp.float32),
+        ],
+        axis=0,
+    )
+    phase = pltpu.roll(phase, rows - lax.axis_index("grp") * row_share, 1).T[:row_share]
+    phase = jnp.concatenate([phase.astype(jnp.int32)] * n_tm, axis=0)
+    edge = share_pad - LANES
+    codes = jnp.concatenate([codes[:, :edge], codes[:, edge:] + phase], axis=1)
     for m in range(n_tm):
         block = codes[m * row_share : (m + 1) * row_share].astype(jnp.int16)
         for g in range(n_grp):
@@ -188,22 +226,62 @@
     wait_all(stores)
 
 
+def surrogate_turns(frames, last_freq, phases, place_ref):
+    surr = phases[0].shape[0]
+    freq_pad = place_ref.shape[1]
+    digits = []
+    for phase in phases:
+        parts = [phase >> 8, (phase >> 4) & 15, phase & 15]
+        digits.append(jnp.concatenate(parts, axis=0).astype(jnp.float32))
+    digits = jnp.concatenate(digits, axis=1).astype(FLOAT8)
+    placed = jnp.dot(digits, place_ref[...], preferred_element_type=jnp.float32)
+    angle = placed[:surr] * 256.0 + placed[surr : 2 * surr] * 16.0 + placed[2 * surr :]
+    angle = angle * (2.0 * math.pi / frames)
+    freq = lax.broadcasted_iota(jnp.int32, (1, freq_pad), 1)
+    weight = jnp.where(freq == last_freq, 1.0 / frames, 2.0 / frames)
+    return jnp.cos(angle) * weight, jnp.sin(angle) * weight
+
+
+def rotate(frames, last_freq, spec_ref, turn_ref, rot_ref, scale_ref):
+    rows = spec_ref.shape[0]
+    surr, freq_pad = turn_ref.shape[0] // 2, turn_ref.shape[1]
+    spec_cos = spec_ref[:, :freq_pad]
+    spec_sin = spec_ref[:, freq_pad:]
+    freq = lax.broadcasted_iota(jnp.int32, (1, freq_pad), 1)
+    pair = jnp.where(freq != last_freq, (2.0 / frames) ** 2 * (frames / 2.0), 0.0)
+    common = jnp.sum((spec_cos * spec_cos + spec_sin * spec_sin) * pair, axis=1, keepdims=True)
+    block = last_freq // LANES * LANES
+    last = jnp.where(freq[:, block : block + LANES] == last_freq, float(frames), 0.0)
+    for s in range(surr):
+        cos_row = turn_ref[pl.ds(s, 1), :]
+        sin_row = turn_ref[pl.ds(surr + s, 1), :]
+        rot_real = spec_cos * cos_row + spec_sin * sin_row
+        rot_imag = spec_cos * sin_row - spec_sin * cos_row
+        at_last = rot_real[:, block : block + LANES]
+        energy = common + jnp.sum(at_last * at_last * last, axis=1, keepdims=True)
+        scale_ref[:, s : s + 1] = lax.rsqrt(energy + EPSILON) * math.sqrt(frames)
+        span = pl.ds(s * rows, rows)
+        rot_ref[span, :freq_pad] = rot_real.astype(jnp.bfloat16)
+        rot_ref[span, freq_pad:] = (-rot_imag).astype(jnp.bfloat16)
+
+
 def spectrum_kernel(
-    share, codes_hbm, high_hbm, low_hbm, cols_hbm, shift_ref, spec_ref, cols_ref,
-    codes_ref, high, low, sems,
+    share, frames, last_freq, freq_share,
+    codes_ref, high_hbm, low_hbm, place_hbm, cols_hbm, shift_ref,
+    spec_ref, turn_ref, rot_ref, scale_ref, cols_ref,
+    high, low, place, sems,
 ):
     n_tm, rows, share_pad = codes_ref.shape
     freq_pad = high.shape[2]
-    codes_copy = start_copy(codes_hbm, codes_ref, sems.at[0])
     copies = [
         [
-            start_copy(high_hbm.at[q], high.at[q], sems.at[1 + 2 * q]),
-            start_copy(low_hbm.at[q], low.at[q], sems.at[2 + 2 * q]),
+            start_copy(high_hbm.at[q], high.at[q], sems.at[2 * q]),
+            start_copy(low_hbm.at[q], low.at[q], sems.at[1 + 2 * q]),
         ]
         for q in range(2)
     ]
+    place_copy = start_copy(place_hbm, place, sems.at[4])
     cols_copy = start_copy(cols_hbm.at[pl.ds(0, cols_ref.shape[0])], cols_ref, sems.at[5])
-    codes_copy.wait()
     codes = codes_ref[...].reshape(n_tm * rows, share_pad).astype(jnp.int32)
     upper = ((codes + 128) >> 8) << 8
     lower = (codes - upper).astype(jnp.float32)
@@ -234,30 +312,21 @@
             spec_sin += part_sin * shift_cos + part_cos * shift_sin
         spec_ref[:, :freq_pad] = spec_cos
         spec_ref[:, freq_pad:] = spec_sin
+    surr = turn_ref.shape[0] // 2
+    chunks = phase_chunks(freq_share, rows)
+    above = phase_lane(share) % LANES
+    phases = []
+    for m in range(n_tm):
+        block = codes[m * rows : (m + 1) * rows, share_pad - LANES :].astype(jnp.float32).T
+        block = block[above : above + round_up(chunks * surr, 8)].astype(jnp.int32)
+        parts = [block[c * surr : (c + 1) * surr] for c in range(chunks)]
+        phases.append(jnp.concatenate(parts, axis=1))
+    place_copy.wait()
+    turn_cos, turn_sin = surrogate_turns(frames, last_freq, phases, place)
+    turn_ref[pl.ds(0, surr), :] = turn_cos
+    turn_ref[pl.ds(surr, surr), :] = turn_sin
+    rotate(frames, last_freq, spec_ref, turn_ref, rot_ref, scale_ref)
     cols_copy.wait()
-
-
-def rotate(frames, last_freq, spec_ref, turn_ref, rot_ref):
-    rows = spec_ref.shape[0]
-    surr, freq_pad = turn_ref.shape[0] // 2, turn_ref.shape[1]
-    spec_cos = spec_ref[:, :freq_pad]
-    spec_sin = spec_ref[:, freq_pad:]
-    freq = lax.broadcasted_iota(jnp.int32, (1, freq_pad), 1)
-    pair = jnp.where(freq != last_freq, (2.0 / frames) ** 2 * (frames / 2.0), 0.0)
-    last = jnp.where(freq == last_freq, float(frames), 0.0)
-    common = jnp.sum((spec_cos * spec_cos + spec_sin * spec_sin) * pair, axis=1, keepdims=True)
-    scales = []
-    for s in range(surr):
-        cos_row = turn_ref[pl.ds(s, 1), :]
-        sin_row = turn_ref[pl.ds(surr + s, 1), :]
-        rot_real = spec_cos * cos_row + spec_sin * sin_row
-        rot_imag = spec_cos * sin_row - spec_sin * cos_row
-        energy = common + jnp.sum(rot_real * rot_real * last, axis=1, keepdims=True)
-        scales.append(lax.rsqrt(energy + EPSILON) * math.sqrt(frames))
-        span = pl.ds(s * rows, rows)
-        rot_ref[span, :freq_pad] = rot_real.astype(jnp.bfloat16)
-        rot_ref[span, freq_pad:] = (-rot_imag).astype(jnp.bfloat16)
-    return scales
 
 
 def raise_top(top, rot, cols_ref):
@@ -268,38 +337,41 @@
     return top
 
 
-def row_peaks(top, scales):
-    rows = scales[0].shape[0]
+def row_peaks(top, scale_ref, surr):
+    rows = scale_ref.shape[0]
     peaks = [
-        jnp.max((top[s * rows : (s + 1) * rows] * scale).T, axis=0, keepdims=True)
-        for s, scale in enumerate(scales)
+        jnp.max((top[s * rows : (s + 1) * rows] * scale_ref[:, s : s + 1]).T, axis=0, keepdims=True)
+        for s in range(surr)
     ]
     return jnp.concatenate(peaks, axis=0)
 
 
-def first_score_kernel(
-    frames, last_freq, spec_ref, turn_ref, near_ref, cols_hbm, peak_ref, far_ref, rot_ref, sem
-):
-    n_near = near_ref.shape[0]
-    copy = start_copy(cols_hbm.at[pl.ds(n_near, far_ref.shape[0])], far_ref, sem)
-    scales = rotate(frames, last_freq, spec_ref, turn_ref, rot_ref)
+def first_score_kernel(rot_ref, scale_ref, near_ref, cols_hbm, peak_ref, far_ref, sem):
+    copy = start_copy(cols_hbm.at[pl.ds(near_ref.shape[0], far_ref.shape[0])], far_ref, sem)
     rot = rot_ref[...]
     top = raise_top(jnp.zeros((rot.shape[0], LANES), jnp.float32), rot, near_ref)
     copy.wait()
-    peak_ref[...] = row_peaks(raise_top(top, rot, far_ref), scales)
+    peak_ref[...] = row_peaks(raise_top(top, rot, far_ref), scale_ref, peak_ref.shape[0])
 
 
 def second_score_kernel(
-    frames, last_freq, spec_ref, turn_ref, near_ref, far_ref, first_ref, own_ref, best_ref, rot_ref
+    frames, last_freq, spec_ref, turn_ref, near_ref, far_ref, first_ref, own_ref, best_ref,
+    rot_ref, scale_ref,
 ):
-    scales = rotate(frames, last_freq, spec_ref, turn_ref, rot_ref)
+    rotate(frames, last_freq, spec_ref, turn_ref, rot_ref, scale_ref)
     rot = rot_ref[...]
     top = raise_top(jnp.zeros((rot.shape[0], LANES), jnp.float32), rot, near_ref)
-    peaks = row_peaks(raise_top(top, rot, far_ref), scales)
+    peaks = row_peaks(raise_top(top, rot, far_ref), scale_ref, first_ref.shape[0])
     first = first_ref[...]
-    own_ref[0] = first
-    own_ref[1] = peaks
-    best_ref[...] = jnp.broadcast_to(jnp.maximum(first, peaks)[None], best_ref.shape)
+    lane = lax.axis_index("lane")
+    own_ref[lane] = first
+    own_ref[1 - lane] = peaks
+    best = jnp.max(jnp.maximum(first, peaks), axis=1, keepdims=True)
+    lane_of = lax.broadcasted_iota(jnp.int32, (1, 1, best_ref.shape[2]), 2)
+    row = jnp.zeros(lane_of.shape, jnp.float32)
+    for s in range(best.shape[0]):
+        row = jnp.where(lane_of == s, best[s : s + 1].reshape(1, 1, 1), row)
+    best_ref[...] = jnp.broadcast_to(row, best_ref.shape)
 
 
 def tm_exchange(value, n_tm):
@@ -322,7 +394,7 @@
     freqs = phase_index.shape[1] * n_tm
     row_share = verts // n_tm
     rows = n_grp * row_share
-    share_pad = round_up(share, LANES)
+    share_pad = round_up(phase_lane(share) + phase_chunks(freqs // n_tm, rows) * surr, LANES)
     half_pad = round_up(frames // 2, LANES)
     order = Order(freqs)
     last_freq = int(np.argmax(order.freq))
@@ -330,22 +402,13 @@
     limits = pltpu.CompilerParams(vmem_limit_bytes=24 * 2**20)
 
     codes = pl.pallas_call(
-        functools.partial(encode_kernel, share),
+        functools.partial(encode_kernel, share, rows),
         out_shape=jax.ShapeDtypeStruct((n_tm, n_grp, row_share, share_pad), jnp.int16),
-        in_specs=[VMEM],
+        in_specs=[VMEM] * 2,
         out_specs=VMEM,
-    )(slab_series.T)
+    )(slab_series.T, phase_index)
     codes = codes.reshape(n_tm * n_grp, row_share, share_pad)
     received = lax.all_to_all(codes, ("tm", "grp"), 0, 0, tiled=True)
-
-    phase = tm_exchange(phase_index, n_tm)
-    phase = jnp.transpose(phase, (1, 0, 2)).reshape(surr, freqs)
-    angle = phase.astype(jnp.float32) * (2.0 * math.pi / frames)
-    weight = jnp.where(jnp.arange(1, freqs + 1) < freqs, 2.0, 1.0) / frames
-    turn = jnp.concatenate([jnp.cos(angle) * weight, jnp.sin(angle) * weight], axis=0)
-    gap = jnp.zeros((2 * surr, order.half - freqs // 2), jnp.float32)
-    turn = jnp.concatenate([turn[:, 1::2], gap, turn[:, 0::2]], axis=1)
-    turn = jnp.pad(turn, ((0, 0), (0, order.pad - turn.shape[1])))
 
     n_tiles = columns // TILE
     col_high, col_low = column_tables(frames, order)
@@ -369,21 +432,26 @@
         ),
     )(in_hbm(series), in_hbm(col_high), in_hbm(col_low))
 
-    received, cols, turn = lax.optimization_barrier((received, cols, turn))
-    high, low, shift = slab_tables(frames, share, n_tm, order)
+    received, cols = lax.optimization_barrier((received, cols))
+    high, low, shift = slab_tables(frames, share, share_pad, n_tm, order)
+    place = placement(order, freqs, n_tm, rows)
     n_near = n_tiles // 2
-    spec, near = pl.pallas_call(
-        functools.partial(spectrum_kernel, share),
+    rot_shape = pltpu.VMEM((surr * rows, points), jnp.bfloat16)
+    spec, turn, rot, scale, near = pl.pallas_call(
+        functools.partial(spectrum_kernel, share, frames, last_freq, freqs // n_tm),
         out_shape=(
             jax.ShapeDtypeStruct((rows, points), jnp.float32),
+            jax.ShapeDtypeStruct((2 * surr, order.pad), jnp.float32),
+            rot_shape,
+            jax.ShapeDtypeStruct((rows, surr), jnp.float32),
             pltpu.VMEM((n_near, points, TILE), jnp.bfloat16),
         ),
-        in_specs=[HBM] * 4 + [VMEM],
-        out_specs=(VMEM, VMEM),
+        in_specs=[VMEM] + [HBM] * 4 + [VMEM],
+        out_specs=(VMEM,) * 5,
         scratch_shapes=[
-            pltpu.VMEM((n_tm, rows, share_pad), jnp.int16),
             pltpu.VMEM(high.shape, jnp.bfloat16),
             pltpu.VMEM(low.shape, FLOAT8),
+            pltpu.VMEM(place.shape, FLOAT8),
             pltpu.SemaphoreType.DMA((6,)),
         ],
         compiler_params=limits,
@@ -391,44 +459,42 @@
             flops=4 * points * n_tm * share_pad * rows, transcendentals=0, bytes_accessed=0
         ),
     )(
-        in_hbm(received.reshape(n_tm, rows, share_pad)),
-        in_hbm(high), in_hbm(low), in_hbm(cols), shift,
+        received.reshape(n_tm, rows, share_pad),
+        in_hbm(high), in_hbm(low), in_hbm(place), in_hbm(cols), shift,
     )
     other = lax.ppermute(spec, "lane", [(i, (i + 1) % n_lane) for i in range(n_lane)])
     score_cost = pl.CostEstimate(
         flops=2 * points * surr * rows * columns, transcendentals=0, bytes_accessed=0
     )
-    rot_shape = pltpu.VMEM((surr * rows, points), jnp.bfloat16)
     first, far = pl.pallas_call(
-        functools.partial(first_score_kernel, frames, last_freq),
+        first_score_kernel,
         out_shape=(
             jax.ShapeDtypeStruct((surr, rows), jnp.float32),
             pltpu.VMEM((n_tiles - n_near, points, TILE), jnp.bfloat16),
         ),
         in_specs=[VMEM] * 3 + [HBM],
         out_specs=(VMEM, VMEM),
-        scratch_shapes=[rot_shape, pltpu.SemaphoreType.DMA],
+        scratch_shapes=[pltpu.SemaphoreType.DMA],
         compiler_params=limits,
         cost_estimate=score_cost,
-    )(spec, turn, near, in_hbm(cols))
+    )(rot, scale, near, in_hbm(cols))
     n_dev = n_grp * n_lane * n_tm
     own, best = pl.pallas_call(
         functools.partial(second_score_kernel, frames, last_freq),
         out_shape=(
             jax.ShapeDtypeStruct((2, surr, rows), jnp.float32),
-            jax.ShapeDtypeStruct((n_dev, surr, rows), jnp.float32),
+            jax.ShapeDtypeStruct((n_dev, 1, LANES), jnp.float32),
         ),
         in_specs=[VMEM] * 5,
         out_specs=(VMEM, VMEM),
-        scratch_shapes=[rot_shape],
+        scratch_shapes=[rot_shape, pltpu.VMEM((rows, surr), jnp.float32)],
         compiler_params=limits,
         cost_estimate=score_cost,
     )(other, turn, near, far, first)
     every = lax.all_to_all(best, ("grp", "lane", "tm"), 0, 0, tiled=True)
-    peak_all = jnp.max(every, axis=(0, 2))
-
-    own = jnp.where(lax.axis_index("lane") == 0, own, own[::-1])[:n_lane]
-    both = tm_exchange(own, n_tm).reshape(n_tm, n_lane, surr, n_grp, row_share)
+    peak_all = jnp.max(every, axis=(0, 1))[:surr]
+
+    both = tm_exchange(own[:n_lane], n_tm).reshape(n_tm, n_lane, surr, n_grp, row_share)
     tile_peak = jnp.transpose(both, (2, 3, 1, 0, 4)).reshape(surr, -1, 1)
     return tile_peak, peak_all
 

time: 48.3 us -> 45.6 us (0.944)
  local copies, waits for them, and re-layouts: 2.71 us -> 0.95 us
  starting transfers between devices: 15.5 us -> 13.8 us
  waiting for transfers between devices: 6.62 us -> 7.26 us
  Pallas kernels: 21.4 us -> 22 us
    ppermute x2 -> x1, starting transfers between devices: 4.96 us -> 1 us  [tm_exchange(): other = lax.ppermute(value, 'tm', [(0, 1), (1, 0)])]
    all_to_all x1, starting transfers between devices: 5.91 us -> 8.31 us  [body(): received = lax.all_to_all(codes, ('tm', 'grp'), 0, 0, tiled=True)]
    all_to_all x1, waiting for transfers between devices: 0.01 us -> 1.05 us  [body(): received = lax.all_to_all(codes, ('tm', 'grp'), 0, 0, tiled=True)]
    slice x2 -> x0, local copies, waits for them, and re-layouts: 0.77 us -> none  [body(): turn = jnp.concatenate([turn[:, 1::2], gap, turn[:, 0::2]], axis=1)]
    unnamed x6 -> x2, local copies, waits for them, and re-layouts: 0.72 us -> 0.01 us
    pallas_call x3, Pallas kernels: 8.19 us -> 8.72 us  [the longest x1 3.72 us: body(): pl.pallas_call(functools.partial(spectrum_kernel, share, frames, last_fre...]
  transfers between devices with their start and end apart: 5 -> 4, of which waited for: 1 -> 2; matrix products, arithmetic and copies ran while one was open for 5% -> 2% of each run, Pallas kernels for 32% -> 30%
where the time goes in v2:
time: 45.6 us; the launch traced here: 45.3 us
  Pallas kernels  22 us (48%)
  starting transfers between devices  13.8 us (30%)
  waiting for transfers between devices  7.26 us (16%)
  local copies, waits for them, and re-layouts  0.95 us (2%)
  between operations  0.73 us (2%)
  other arithmetic  0.58 us (1%)
    pallas_call x1, Pallas kernels, body(): pl.pallas_call(column_kernel, out_shape=pltpu.HBM((n_tiles, points, TILE)...  10.2 us
    all_to_all x1, starting transfers between devices, body(): received = lax.all_to_all(codes, ('tm', 'grp'), 0, 0, tiled=True)  8.31 us
    all_to_all x1, waiting for transfers between devices, body(): every = lax.all_to_all(best, ('grp', 'lane', 'tm'), 0, 0, tiled=True)  6.2 us
    all_to_all x1, starting transfers between devices, body(): every = lax.all_to_all(best, ('grp', 'lane', 'tm'), 0, 0, tiled=True)  4.42 us
    pallas_call x1, Pallas kernels, body(): pl.pallas_call(functools.partial(spectrum_kernel, share, frames, last_fre...  3.72 us
    pallas_call x1, Pallas kernels, body(): pl.pallas_call(first_score_kernel, out_shape=(jax.ShapeDtypeStruct((surr,...  3.18 us
    pallas_call x1, Pallas kernels, body(): pl.pallas_call(functools.partial(second_score_kernel, frames, last_freq),...  3.04 us
    pallas_call x1, Pallas kernels, body(): pl.pallas_call(functools.partial(encode_kernel, share, rows), out_shape=j...  1.82 us
  transfers between devices with their start and end apart: 4, of which 2 were waited for; matrix products, arithmetic and copies ran while one was open for 2% of the time, Pallas kernels for 30%

profile of v2, /device:TPU:0, one launch (start us, length us, event | category | flops | bytes accessed | tf_op | source)
XLA Modules:
  0.0 45.3 jit_solution(15006765144303625161)
XLA Ops:
  0.6 1.8 %shard_map.104 = s16[2,8,16,640]{3,2,1,0:T(8,128)(2,1)} custom-call(f32[32,600]{1,0:T(8,128)} %bitcast.13, s32[4,300]{1,0:T(4,128)} %phase_ref.1), custom_call_target="tpu_custom_call" | custom-call | tf_op jit(solution)/shard_map/pallas_call | solution.py:404
  2.5 8.3 %all-to-all-start = ((s16[16,16,640]{2,1,0:T(8,128)(2,1)}), s16[16,16,640]{2,1,0:T(8,128)(2,1)S(1)}, u32[]{:S(2)}, u32[]{:S(2)}) async-start(s16[16,16,640]{2,1,0:T(8,128)(2,1)} %bitcast.12), calls=%async_computation | async-start | bytes 655360 | tf_op jit(solution)/shard_map/all_to_all | solution.py:411
  10.8 0.0 copy-start
  10.8 10.2 %shard_map.105.cols_hbm = bf16[6,1280,256]{2,1,0:T(8,128)(2,1)} custom-call(bf16[1200,1536]{1,0:T(8,128)(2,1)} %series_hbm.1, bf16[2,608,640]{2,1,0:T(8,128)(2,1)} %constant.20.clone.high_hbm, f8e4m3fn[2,608,1280]{2,1,0:T(32,128)(4,1)} %constant.21.clone.low_hbm), custom_call_target="tpu_custom_call" | custom-call | flops 7077888000 | tf_op jit(solution)/shard_map/pallas_call | solution.py:415
  21.0 1.0 %all-to-all-done = s16[16,16,640]{2,1,0:T(8,128)(2,1)S(1)} async-done(((s16[16,16,640]{2,1,0:T(8,128)(2,1)}), s16[16,16,640]{2,1,0:T(8,128)(2,1)S(1)}, u32[]{:S(2)}, u32[]{:S(2)}) %all-to-all-start) | async-done | bytes 327712 | tf_op jit(solution)/shard_map/all_to_all | solution.py:411
  22.1 0.0 copy-done
  22.1 3.7 %shard_map.106 = (f32[128,1280]{1,0:T(8,128)S(1)}, f32[8,640]{1,0:T(8,128)S(1)}, bf16[512,1280]{1,0:T(8,128)(2,1)S(1)}, f32[128,4]{1,0:T(8,128)S(1)}, bf16[3,1280,256]{2,1,0:T(8,128)(2,1)S(1)}) custom-call(s16[2,128,640]{2,1,0:T(8,128)(2,1)S(1)} %bitcast.10, bf16[2,640,640]{2,1,0:T(8,128)(2,1)} %constant.22.clone.high_hbm, ...), custom_call_target="tpu_custom_call" | custom-call | flops 838860800 | tf_op jit(solution)/shard_map/pallas_call | solution.py:440
  25.8 0.1 collective-permute-start
  25.9 3.2 %shard_map.107 = (f32[4,128]{1,0:T(4,128)S(1)}, bf16[3,1280,256]{2,1,0:T(8,128)(2,1)S(1)}) custom-call(bf16[512,1280]{1,0:T(8,128)(2,1)S(1)} %get-tuple-element.18.rot_ref, f32[128,4]{1,0:T(8,128)S(1)} %get-tuple-element.19.scale_ref, bf16[3,1280,256]{2,1,0:T(8,128)(2,1)S(1)} %get-tuple-element.17.near_ref, bf16[6,1280,256]{2,1,0:T(8,128)(2,1)} %shard_map.105.cols_hbm), custom_call_target="tpu_custom_call" | custom-call | flops 2013265920 | tf_op jit(solution)/shard_map/pallas_call | solution.py:469
  29.1 0.0 collective-permute-done.spec_ref
  29.1 3.0 %shard_map.108 = (f32[2,4,128]{2,1,0:T(4,128)S(1)}, f32[32,1,128]{2,1,0:T(1,128)}) custom-call(f32[128,1280]{1,0:T(8,128)S(1)} %collective-permute-done.spec_ref, f32[8,640]{1,0:T(8,128)S(1)} %get-tuple-element.16.turn_ref, bf16[3,1280,256]{2,1,0:T(8,128)(2,1)S(1)} %get-tuple-element.17.near_ref, bf16[3,1280,256]{2,1,0:T(8,128)(2,1)S(1)} %get-tuple-element.20.far_ref, ...), custom_call_target="tpu_custom_call" | custom-call | flops 2013265920 | tf_op jit(solution)/shard_map/pallas_call | solution.py:482
  32.1 1.0 %collective-permute-start.1 = (f32[2,4,128]{2,1,0:T(4,128)S(1)}, f32[2,4,128]{2,1,0:T(4,128)S(1)}, u32[]{:S(2)}, u32[]{:S(2)}) collective-permute-start(f32[2,4,128]{2,1,0:T(4,128)S(1)} %get-tuple-element.22), channel_id=1, source_target_pairs={{0,1},{1,0},{2,3},{3,2},{4,5},{5,4},{6,7},{7,6},{8,9},{9,8},{10,11... | collective-permute-start | bytes 12296 | tf_op jit(solution)/shard_map/ppermute | solution.py:379
  33.1 4.4 %all-to-all-start.1 = ((f32[32,1,128]{2,1,0:T(1,128)}), f32[32,1,128]{2,1,0:T(1,128)S(1)}, u32[]{:S(2)}, u32[]{:S(2)}) async-start(f32[32,1,128]{2,1,0:T(1,128)} %get-tuple-element.23), calls=%async_computation.1 | async-start | bytes 32768 | tf_op jit(solution)/shard_map/all_to_all | solution.py:494
  37.6 0.0 collective-permute-done.1
  37.6 0.1 stack.10
  37.7 0.1 stack.9
  37.8 0.1 copy.11
  37.8 0.7 %reshape.20 = f32[4,512,1]{1,2,0:T(1,128)} reshape(f32[4,8,2,2,16]{4,3,2,1,0:T(2,128)S(1)} %copy.11) | data formatting | bytes 16384 | tf_op jit(solution)/shard_map/reshape | solution.py:498
  38.6 6.2 %all-to-all-done.1 = f32[32,1,128]{2,1,0:T(1,128)S(1)} async-done(((f32[32,1,128]{2,1,0:T(1,128)}), f32[32,1,128]{2,1,0:T(1,128)S(1)}, u32[]{:S(2)}, u32[]{:S(2)}) %all-to-all-start.1) | async-done | bytes 16416 | tf_op jit(solution)/shard_map/all_to_all | solution.py:494
  44.8 0.6 %reduce_max.9 = f32[128]{0:T(128)} reduce(f32[32,1,128]{2,1,0:T(1,128)S(1)} %all-to-all-done.1, f32[]{:T(128)} %constant.8.clone.1), dimensions={0,1}, to_apply=%region_0.0 | reduce | flops 3968 | bytes 16900 | tf_op jit(solution)/shard_map/reduce_max | solution.py:495
  (2 shorter events, 0.0 us)
Async XLA Ops:
  2.5 19.6 %all-to-all-start = ((s16[16,16,640]{2,1,0:T(8,128)(2,1)}), s16[16,16,640]{2,1,0:T(8,128)(2,1)S(1)}, u32[]{:S(2)}, u32[]{:S(2)}) async-start(s16[16,16,640]{2,1,0:T(8,128)(2,1)} %bitcast.12), calls=%async_computation | async-start | bytes 655360 | tf_op jit(solution)/shard_map/all_to_all | solution.py:411
  10.8 11.3 %copy-start = (f32[5,1280]{1,0:T(8,128)S(1)}, f32[5,1280]{1,0:T(8,128)}, u32[]{:S(2)}) copy-start(f32[5,1280]{1,0:T(8,128)} %constant.24.clone.shift_ref) | copy-start | bytes 76804
  25.8 3.3 %collective-permute-start = (f32[128,1280]{1,0:T(8,128)S(1)}, f32[128,1280]{1,0:T(8,128)S(1)}, u32[]{:S(2)}, u32[]{:S(2)}) collective-permute-start(f32[128,1280]{1,0:T(8,128)S(1)} %get-tuple-element.15), channel_id=1, source_target_pairs={{0,2},{2,0},{1,3},{3,1},{4,6},{6,4},{5,7},{7,5},{8,10},{10,8},{9,1... | collective-permute-start | bytes 1966088 | tf_op jit(solution)/shard_map/ppermute | solution.py:465
  32.1 5.4 %collective-permute-start.1 = (f32[2,4,128]{2,1,0:T(4,128)S(1)}, f32[2,4,128]{2,1,0:T(4,128)S(1)}, u32[]{:S(2)}, u32[]{:S(2)}) collective-permute-start(f32[2,4,128]{2,1,0:T(4,128)S(1)} %get-tuple-element.22), channel_id=1, source_target_pairs={{0,1},{1,0},{2,3},{3,2},{4,5},{5,4},{6,7},{7,6},{8,9},{9,8},{10,11... | collective-permute-start | bytes 12296 | tf_op jit(solution)/shard_map/ppermute | solution.py:379
  33.1 11.6 %all-to-all-start.1 = ((f32[32,1,128]{2,1,0:T(1,128)}), f32[32,1,128]{2,1,0:T(1,128)S(1)}, u32[]{:S(2)}, u32[]{:S(2)}) async-start(f32[32,1,128]{2,1,0:T(1,128)} %get-tuple-element.23), calls=%async_computation.1 | async-start | bytes 32768 | tf_op jit(solution)/shard_map/all_to_all | solution.py:494

commit v3 on v2

--- a/solution.py
+++ b/solution.py
@@ -139,7 +139,9 @@
         ],
         axis=0,
     )
-    phase = pltpu.roll(phase, rows - lax.axis_index("grp") * row_share, 1).T[:row_share]
+    group = lax.axis_index("grp")
+    place = jnp.where(lax.axis_index("lane") == 0, group, n_grp - 1 - group)
+    phase = pltpu.roll(phase, rows - place * row_share, 1).T[:row_share]
     phase = jnp.concatenate([phase.astype(jnp.int32)] * n_tm, axis=0)
     edge = share_pad - LANES
     codes = jnp.concatenate([codes[:, :edge], codes[:, edge:] + phase], axis=1)
@@ -235,11 +237,26 @@
         digits.append(jnp.concatenate(parts, axis=0).astype(jnp.float32))
     digits = jnp.concatenate(digits, axis=1).astype(FLOAT8)
     placed = jnp.dot(digits, place_ref[...], preferred_element_type=jnp.float32)
-    angle = placed[:surr] * 256.0 + placed[surr : 2 * surr] * 16.0 + placed[2 * surr :]
-    angle = angle * (2.0 * math.pi / frames)
+    turn = placed[:surr] * 256.0 + placed[surr : 2 * surr] * 16.0 + placed[2 * surr :]
     freq = lax.broadcasted_iota(jnp.int32, (1, freq_pad), 1)
     weight = jnp.where(freq == last_freq, 1.0 / frames, 2.0 / frames)
-    return jnp.cos(angle) * weight, jnp.sin(angle) * weight
+    cos, sin = turn_waves(frames, turn)
+    return cos * weight, sin * weight
+
+
+def turn_waves(frames, turn):
+    quarter = frames / 4
+    quadrant = jnp.floor(turn * (1.0 / quarter) + 0.5)
+    x = (turn - quadrant * quarter) * (2.0 * math.pi / frames)
+    y = x * x
+    cos = 1.0 + y * (-1 / 2 + y * (1 / 24 + y * (-1 / 720 + y * (1 / 40320 - y * (1 / 3628800)))))
+    sin = x * (1.0 + y * (-1 / 6 + y * (1 / 120 + y * (-1 / 5040 + y * (1 / 362880)))))
+    odd = (quadrant == 1.0) | (quadrant == 3.0)
+    left = (quadrant == 1.0) | (quadrant == 2.0)
+    down = (quadrant == 2.0) | (quadrant == 3.0)
+    near = jnp.where(odd, sin, cos)
+    far = jnp.where(odd, cos, sin)
+    return jnp.where(left, -near, near), jnp.where(down, -far, far)
 
 
 def rotate(frames, last_freq, spec_ref, turn_ref, rot_ref, scale_ref):
@@ -268,11 +285,12 @@
 def spectrum_kernel(
     share, frames, last_freq, freq_share,
     codes_ref, high_hbm, low_hbm, place_hbm, cols_hbm, shift_ref,
-    spec_ref, turn_ref, rot_ref, scale_ref, cols_ref,
+    spec_ref, turn_ref, cols_ref,
     high, low, place, sems,
 ):
     n_tm, rows, share_pad = codes_ref.shape
     freq_pad = high.shape[2]
+    place_copy = start_copy(place_hbm, place, sems.at[4])
     copies = [
         [
             start_copy(high_hbm.at[q], high.at[q], sems.at[2 * q]),
@@ -280,7 +298,6 @@
         ]
         for q in range(2)
     ]
-    place_copy = start_copy(place_hbm, place, sems.at[4])
     cols_copy = start_copy(cols_hbm.at[pl.ds(0, cols_ref.shape[0])], cols_ref, sems.at[5])
     codes = codes_ref[...].reshape(n_tm * rows, share_pad).astype(jnp.int32)
     upper = ((codes + 128) >> 8) << 8
@@ -291,6 +308,17 @@
     digits = [codes[:, share + p : share + p + 1] for p in range(6)]
     step = join_digits(*digits[:3]) * (1.0 / CODE_TOP)
     mean = join_digits(*digits[3:])
+    surr = turn_ref.shape[0] // 2
+    chunks = phase_chunks(freq_share, rows)
+    above = phase_lane(share) % LANES
+    phases = []
+    for m in range(n_tm):
+        block = codes[m * rows : (m + 1) * rows, share_pad - LANES :].astype(jnp.float32).T
+        block = block[above : above + round_up(chunks * surr, 8)].astype(jnp.int32)
+        parts = [block[c * surr : (c + 1) * surr] for c in range(chunks)]
+        phases.append(jnp.concatenate(parts, axis=1))
+    place_copy.wait()
+    turn_cos, turn_sin = surrogate_turns(frames, last_freq, phases, place)
     parts = []
     for q in range(2):
         wait_all(copies[q])
@@ -312,20 +340,8 @@
             spec_sin += part_sin * shift_cos + part_cos * shift_sin
         spec_ref[:, :freq_pad] = spec_cos
         spec_ref[:, freq_pad:] = spec_sin
-    surr = turn_ref.shape[0] // 2
-    chunks = phase_chunks(freq_share, rows)
-    above = phase_lane(share) % LANES
-    phases = []
-    for m in range(n_tm):
-        block = codes[m * rows : (m + 1) * rows, share_pad - LANES :].astype(jnp.float32).T
-        block = block[above : above + round_up(chunks * surr, 8)].astype(jnp.int32)
-        parts = [block[c * surr : (c + 1) * surr] for c in range(chunks)]
-        phases.append(jnp.concatenate(parts, axis=1))
-    place_copy.wait()
-    turn_cos, turn_sin = surrogate_turns(frames, last_freq, phases, place)
     turn_ref[pl.ds(0, surr), :] = turn_cos
     turn_ref[pl.ds(surr, surr), :] = turn_sin
-    rotate(frames, last_freq, spec_ref, turn_ref, rot_ref, scale_ref)
     cols_copy.wait()
 
 
@@ -346,8 +362,11 @@
     return jnp.concatenate(peaks, axis=0)
 
 
-def first_score_kernel(rot_ref, scale_ref, near_ref, cols_hbm, peak_ref, far_ref, sem):
+def first_score_kernel(
+    frames, last_freq, spec_ref, turn_ref, near_ref, cols_hbm, peak_ref, far_ref, rot_ref, scale_ref, sem
+):
     copy = start_copy(cols_hbm.at[pl.ds(near_ref.shape[0], far_ref.shape[0])], far_ref, sem)
+    rotate(frames, last_freq, spec_ref, turn_ref, rot_ref, scale_ref)
     rot = rot_ref[...]
     top = raise_top(jnp.zeros((rot.shape[0], LANES), jnp.float32), rot, near_ref)
     copy.wait()
@@ -382,6 +401,11 @@
     return lax.all_gather(value, "tm")
 
 
+def lane_groups(n_grp, n_lane, n_tm):
+    index = np.arange(n_grp * n_lane * n_tm).reshape(n_grp, n_lane, n_tm)
+    return [index[:: 1 - 2 * lane, lane].T.reshape(-1).tolist() for lane in range(n_lane)]
+
+
 def in_hbm(array):
     return pltpu.with_memory_space_constraint(array, pltpu.HBM)
 
@@ -403,12 +427,16 @@
 
     codes = pl.pallas_call(
         functools.partial(encode_kernel, share, rows),
-        out_shape=jax.ShapeDtypeStruct((n_tm, n_grp, row_share, share_pad), jnp.int16),
+        out_shape=pltpu.VMEM((n_tm, n_grp, row_share, share_pad), jnp.int16),
         in_specs=[VMEM] * 2,
         out_specs=VMEM,
-    )(slab_series.T, phase_index)
+        compiler_params=limits,
+    )(in_hbm(slab_series.T), in_hbm(phase_index))
     codes = codes.reshape(n_tm * n_grp, row_share, share_pad)
-    received = lax.all_to_all(codes, ("tm", "grp"), 0, 0, tiled=True)
+    received = lax.all_to_all(
+        codes, ("grp", "lane", "tm"), 0, 0, tiled=True,
+        axis_index_groups=lane_groups(n_grp, n_lane, n_tm),
+    )
 
     n_tiles = columns // TILE
     col_high, col_low = column_tables(frames, order)
@@ -437,17 +465,15 @@
     place = placement(order, freqs, n_tm, rows)
     n_near = n_tiles // 2
     rot_shape = pltpu.VMEM((surr * rows, points), jnp.bfloat16)
-    spec, turn, rot, scale, near = pl.pallas_call(
+    spec, turn, near = pl.pallas_call(
         functools.partial(spectrum_kernel, share, frames, last_freq, freqs // n_tm),
         out_shape=(
             jax.ShapeDtypeStruct((rows, points), jnp.float32),
             jax.ShapeDtypeStruct((2 * surr, order.pad), jnp.float32),
-            rot_shape,
-            jax.ShapeDtypeStruct((rows, surr), jnp.float32),
             pltpu.VMEM((n_near, points, TILE), jnp.bfloat16),
         ),
         in_specs=[VMEM] + [HBM] * 4 + [VMEM],
-        out_specs=(VMEM,) * 5,
+        out_specs=(VMEM,) * 3,
         scratch_shapes=[
             pltpu.VMEM(high.shape, jnp.bfloat16),
             pltpu.VMEM(low.shape, FLOAT8),
@@ -467,17 +493,17 @@
         flops=2 * points * surr * rows * columns, transcendentals=0, bytes_accessed=0
     )
     first, far = pl.pallas_call(
-        first_score_kernel,
+        functools.partial(first_score_kernel, frames, last_freq),
         out_shape=(
             jax.ShapeDtypeStruct((surr, rows), jnp.float32),
             pltpu.VMEM((n_tiles - n_near, points, TILE), jnp.bfloat16),
         ),
         in_specs=[VMEM] * 3 + [HBM],
         out_specs=(VMEM, VMEM),
-        scratch_shapes=[pltpu.SemaphoreType.DMA],
+        scratch_shapes=[rot_shape, pltpu.VMEM((rows, surr), jnp.float32), pltpu.SemaphoreType.DMA],
         compiler_params=limits,
         cost_estimate=score_cost,
-    )(rot, scale, near, in_hbm(cols))
+    )(spec, turn, near, in_hbm(cols))
     n_dev = n_grp * n_lane * n_tm
     own, best = pl.pallas_call(
         functools.partial(second_score_kernel, frames, last_freq),
@@ -495,6 +521,7 @@
     peak_all = jnp.max(every, axis=(0, 1))[:surr]
 
     both = tm_exchange(own[:n_lane], n_tm).reshape(n_tm, n_lane, surr, n_grp, row_share)
+    both = jnp.concatenate([both[:, :1], both[:, 1:, :, ::-1]], axis=1)
     tile_peak = jnp.transpose(both, (2, 3, 1, 0, 4)).reshape(surr, -1, 1)
     return tile_peak, peak_all
 

time: 45.6 us -> 45 us (0.987)
  waiting for transfers between devices: 7.26 us -> 6.16 us
  starting transfers between devices: 13.8 us -> 14.8 us
  Pallas kernels: 22 us -> 21.4 us
    all_to_all x1, waiting for transfers between devices: 1.05 us -> 0.01 us  [body(): lax.all_to_all(codes, ('grp', 'lane', 'tm'), 0, 0, tiled=True, axis_index...]
    pallas_call x1, Pallas kernels: 3.72 us -> 3.06 us  [body(): pl.pallas_call(functools.partial(spectrum_kernel, share, frames, last_fre...]
    ppermute x1, starting transfers between devices: 0.07 us -> 0.65 us  [body(): lax.ppermute(spec, 'lane', [(i, (i + 1) % n_lane) for i in range(n_lane)])]
    ppermute x1, starting transfers between devices: 1 us -> 1.52 us  [tm_exchange(): other = lax.ppermute(value, 'tm', [(0, 1), (1, 0)])]
  transfers between devices with their start and end apart: 4 -> 4, of which waited for: 2 -> 1; matrix products, arithmetic and copies ran while one was open for 2% -> 2% of each run, Pallas kernels for 30% -> 30%
where the time goes in v3:
time: 45 us; the launch traced here: 44.7 us
  Pallas kernels  21.4 us (48%)
  starting transfers between devices  14.8 us (33%)
  waiting for transfers between devices  6.16 us (14%)
  local copies, waits for them, and re-layouts  0.98 us (2%)
  between operations  0.76 us (2%)
  other arithmetic  0.57 us (1%)
    pallas_call x1, Pallas kernels, body(): pl.pallas_call(column_kernel, out_shape=pltpu.HBM((n_tiles, points, TILE)...  10.2 us
    all_to_all x1, starting transfers between devices, body(): lax.all_to_all(codes, ('grp', 'lane', 'tm'), 0, 0, tiled=True, axis_index...  8.31 us
    all_to_all x1, waiting for transfers between devices, body(): every = lax.all_to_all(best, ('grp', 'lane', 'tm'), 0, 0, tiled=True)  6.15 us
    all_to_all x1, starting transfers between devices, body(): every = lax.all_to_all(best, ('grp', 'lane', 'tm'), 0, 0, tiled=True)  4.36 us
    pallas_call x1, Pallas kernels, body(): pl.pallas_call(functools.partial(first_score_kernel, frames, last_freq),...  3.18 us
    pallas_call x1, Pallas kernels, body(): pl.pallas_call(functools.partial(spectrum_kernel, share, frames, last_fre...  3.06 us
    pallas_call x1, Pallas kernels, body(): pl.pallas_call(functools.partial(second_score_kernel, frames, last_freq),...  3.05 us
    pallas_call x1, Pallas kernels, body(): pl.pallas_call(functools.partial(encode_kernel, share, rows), out_shape=p...  1.82 us
  transfers between devices with their start and end apart: 4, of which 1 were waited for; matrix products, arithmetic and copies ran while one was open for 2% of the time, Pallas kernels for 30%

profile of v3, /device:TPU:0, one launch (start us, length us, event | category | flops | bytes accessed | tf_op | source)
XLA Modules:
  0.0 44.7 jit_solution(6715979533168382066)
XLA Ops:
  0.6 1.8 %shard_map.104 = s16[2,8,16,640]{3,2,1,0:T(8,128)(2,1)} custom-call(f32[32,600]{1,0:T(8,128)} %bitcast.12, s32[4,300]{1,0:T(4,128)} %phase_ref.1), custom_call_target="tpu_custom_call" | custom-call | tf_op jit(solution)/shard_map/pallas_call | solution.py:428
  2.5 8.3 %all-to-all-start = ((s16[16,16,640]{2,1,0:T(8,128)(2,1)}), s16[16,16,640]{2,1,0:T(8,128)(2,1)S(1)}, u32[]{:S(2)}, u32[]{:S(2)}) async-start(s16[16,16,640]{2,1,0:T(8,128)(2,1)} %bitcast.1), calls=%async_computation | async-start | bytes 655360 | tf_op jit(solution)/shard_map/all_to_all | solution.py:436
  10.8 0.0 copy-start
  10.8 10.2 %shard_map.105.cols_hbm = bf16[6,1280,256]{2,1,0:T(8,128)(2,1)} custom-call(bf16[1200,1536]{1,0:T(8,128)(2,1)} %series_hbm.1, bf16[2,608,640]{2,1,0:T(8,128)(2,1)} %constant.20.clone.high_hbm, f8e4m3fn[2,608,1280]{2,1,0:T(32,128)(4,1)} %constant.21.clone.low_hbm), custom_call_target="tpu_custom_call" | custom-call | flops 7077888000 | tf_op jit(solution)/shard_map/pallas_call | solution.py:443
  21.0 0.0 all-to-all-done
  21.0 0.0 copy-done
  21.1 3.1 %shard_map.106 = (f32[128,1280]{1,0:T(8,128)S(1)}, f32[8,640]{1,0:T(8,128)S(1)}, bf16[3,1280,256]{2,1,0:T(8,128)(2,1)S(1)}) custom-call(s16[2,128,640]{2,1,0:T(8,128)(2,1)S(1)} %bitcast.10, bf16[2,640,640]{2,1,0:T(8,128)(2,1)} %constant.22.clone.high_hbm, f8e4m3fn[2,1280,640]{2,1,0:T(32,128)(4,1)} %constant.23.clone.low_hbm, ...), custom_call_target="tpu_custom_call" | custom-call | flops 838860800 | tf_op jit(solution)/shard_map/pallas_call | solution.py:468
  24.1 0.6 %collective-permute-start = (f32[128,1280]{1,0:T(8,128)S(1)}, f32[128,1280]{1,0:T(8,128)S(1)}, u32[]{:S(2)}, u32[]{:S(2)}) collective-permute-start(f32[128,1280]{1,0:T(8,128)S(1)} %get-tuple-element.13.spec_ref), channel_id=1, source_target_pairs={{0,2},{2,0},{1,3},{3,1},{4,6},{6,4},{5,7},{7,5},{8,10},{10,8},{9,1... | collective-permute-start | bytes 1966088 | tf_op jit(solution)/shard_map/ppermute | solution.py:491
  24.8 3.2 %shard_map.107 = (f32[4,128]{1,0:T(4,128)S(1)}, bf16[3,1280,256]{2,1,0:T(8,128)(2,1)S(1)}) custom-call(f32[128,1280]{1,0:T(8,128)S(1)} %get-tuple-element.13.spec_ref, f32[8,640]{1,0:T(8,128)S(1)} %get-tuple-element.14.turn_ref, bf16[3,1280,256]{2,1,0:T(8,128)(2,1)S(1)} %get-tuple-element.15.near_ref, bf16[6,1280,256]{2,1,0:T(8,128)(2,1)} %shard_map.105.cols_hbm), custom_call_target="tpu_custom_call" | custom-call | flops 2013265920 | tf_op jit(solution)/shard_map/pallas_call | solution.py:495
  28.0 0.0 collective-permute-done.spec_ref
  28.0 3.1 %shard_map.108 = (f32[2,4,128]{2,1,0:T(4,128)S(1)}, f32[32,1,128]{2,1,0:T(1,128)}) custom-call(f32[128,1280]{1,0:T(8,128)S(1)} %collective-permute-done.spec_ref, f32[8,640]{1,0:T(8,128)S(1)} %get-tuple-element.14.turn_ref, bf16[3,1280,256]{2,1,0:T(8,128)(2,1)S(1)} %get-tuple-element.15.near_ref, bf16[3,1280,256]{2,1,0:T(8,128)(2,1)S(1)} %get-tuple-element.16.far_ref, ...), custom_call_target="tpu_custom_call" | custom-call | flops 2013265920 | tf_op jit(solution)/shard_map/pallas_call | solution.py:508
  31.0 1.5 %collective-permute-start.1 = (f32[2,4,128]{2,1,0:T(4,128)S(1)}, f32[2,4,128]{2,1,0:T(4,128)S(1)}, u32[]{:S(2)}, u32[]{:S(2)}) collective-permute-start(f32[2,4,128]{2,1,0:T(4,128)S(1)} %get-tuple-element.18), channel_id=1, source_target_pairs={{0,1},{1,0},{2,3},{3,2},{4,5},{5,4},{6,7},{7,6},{8,9},{9,8},{10,11... | collective-permute-start | bytes 12296 | tf_op jit(solution)/shard_map/ppermute | solution.py:398
  32.5 4.4 %all-to-all-start.1 = ((f32[32,1,128]{2,1,0:T(1,128)}), f32[32,1,128]{2,1,0:T(1,128)S(1)}, u32[]{:S(2)}, u32[]{:S(2)}) async-start(f32[32,1,128]{2,1,0:T(1,128)} %get-tuple-element.19), calls=%async_computation.1 | async-start | bytes 32768 | tf_op jit(solution)/shard_map/all_to_all | solution.py:520
  36.9 0.0 collective-permute-done.1
  36.9 0.1 stack.9
  37.0 0.1 stack.10
  37.2 0.1 copy.11
  37.2 0.7 %reshape.20 = f32[4,512,1]{1,2,0:T(1,128)} reshape(f32[4,8,2,2,16]{4,3,2,1,0:T(2,128)S(1)} %copy.11) | data formatting | bytes 16384 | tf_op jit(solution)/shard_map/reshape | solution.py:525
  38.0 6.2 %all-to-all-done.1 = f32[32,1,128]{2,1,0:T(1,128)S(1)} async-done(((f32[32,1,128]{2,1,0:T(1,128)}), f32[32,1,128]{2,1,0:T(1,128)S(1)}, u32[]{:S(2)}, u32[]{:S(2)}) %all-to-all-start.1) | async-done | bytes 16416 | tf_op jit(solution)/shard_map/all_to_all | solution.py:520
  44.1 0.6 %reduce_max.9 = f32[128]{0:T(128)} reduce(f32[32,1,128]{2,1,0:T(1,128)S(1)} %all-to-all-done.1, f32[]{:T(128)} %constant.8.clone.1), dimensions={0,1}, to_apply=%region_0.0 | reduce | flops 3968 | bytes 16900 | tf_op jit(solution)/shard_map/reduce_max | solution.py:521
  (6 shorter events, 0.0 us)
Async XLA Ops:
  2.5 18.6 %all-to-all-start = ((s16[16,16,640]{2,1,0:T(8,128)(2,1)}), s16[16,16,640]{2,1,0:T(8,128)(2,1)S(1)}, u32[]{:S(2)}, u32[]{:S(2)}) async-start(s16[16,16,640]{2,1,0:T(8,128)(2,1)} %bitcast.1), calls=%async_computation | async-start | bytes 655360 | tf_op jit(solution)/shard_map/all_to_all | solution.py:436
  10.8 10.3 %copy-start = (f32[5,1280]{1,0:T(8,128)S(1)}, f32[5,1280]{1,0:T(8,128)}, u32[]{:S(2)}) copy-start(f32[5,1280]{1,0:T(8,128)} %constant.24.clone.shift_ref) | copy-start | bytes 76804
  24.1 3.8 %collective-permute-start = (f32[128,1280]{1,0:T(8,128)S(1)}, f32[128,1280]{1,0:T(8,128)S(1)}, u32[]{:S(2)}, u32[]{:S(2)}) collective-permute-start(f32[128,1280]{1,0:T(8,128)S(1)} %get-tuple-element.13.spec_ref), channel_id=1, source_target_pairs={{0,2},{2,0},{1,3},{3,1},{4,6},{6,4},{5,7},{7,5},{8,10},{10,8},{9,1... | collective-permute-start | bytes 1966088 | tf_op jit(solution)/shard_map/ppermute | solution.py:491
  31.0 5.9 %collective-permute-start.1 = (f32[2,4,128]{2,1,0:T(4,128)S(1)}, f32[2,4,128]{2,1,0:T(4,128)S(1)}, u32[]{:S(2)}, u32[]{:S(2)}) collective-permute-start(f32[2,4,128]{2,1,0:T(4,128)S(1)} %get-tuple-element.18), channel_id=1, source_target_pairs={{0,1},{1,0},{2,3},{3,2},{4,5},{5,4},{6,7},{7,6},{8,9},{9,8},{10,11... | collective-permute-start | bytes 12296 | tf_op jit(solution)/shard_map/ppermute | solution.py:398
  32.5 11.6 %all-to-all-start.1 = ((f32[32,1,128]{2,1,0:T(1,128)}), f32[32,1,128]{2,1,0:T(1,128)S(1)}, u32[]{:S(2)}, u32[]{:S(2)}) async-start(f32[32,1,128]{2,1,0:T(1,128)} %get-tuple-element.19), calls=%async_computation.1 | async-start | bytes 32768 | tf_op jit(solution)/shard_map/all_to_all | solution.py:520

commit v4 on v3

--- a/solution.py
+++ b/solution.py
@@ -15,9 +15,8 @@
 CODE_TOP = 32767.0
 LOW_SCALE = 2.0**14
 COARSE_SCALE = 2.0**6
+CODE_SCALE = COARSE_SCALE / LOW_SCALE
 COL_SCALE = 2.0**8
-COL_REST_SCALE = LOW_SCALE * COL_SCALE / COARSE_SCALE
-CODE_SCALE = COARSE_SCALE / LOW_SCALE
 FLOAT8 = jnp.float8_e4m3fn
 VMEM = pl.BlockSpec(memory_space=pltpu.VMEM)
 HBM = pl.BlockSpec(memory_space=pltpu.HBM)
@@ -28,10 +27,10 @@
     return -(-value // unit) * unit
 
 
-def split_table(table, axis):
+def split_table(table, axis, low_scale, coarse_scale):
     high = table.astype(ml_dtypes.bfloat16)
-    low = (table - high.astype(np.float64)) * LOW_SCALE
-    low = np.concatenate([low, table * COARSE_SCALE], axis=axis).astype(ml_dtypes.float8_e4m3fn)
+    low = (table - high.astype(np.float64)) * low_scale
+    low = np.concatenate([low, table * coarse_scale], axis=axis).astype(ml_dtypes.float8_e4m3fn)
     return jnp.asarray(np.ascontiguousarray(high)), jnp.asarray(np.ascontiguousarray(low))
 
 
@@ -57,12 +56,12 @@
     half_pad = round_up(frames // 2, LANES)
     wave = pad_last(order.wave(np.arange(frames // 2), frames), half_pad)[:, : 2 * order.half]
     wave = wave.reshape(2, 2, order.half, half_pad).transpose(1, 0, 2, 3)
-    return split_table(wave.reshape(2, 2 * order.half, half_pad), 2)
+    return split_table(wave.reshape(2, 2 * order.half, half_pad) * COL_SCALE, 2, 1.0, 1.0)
 
 
 def slab_tables(frames, share, share_pad, n_tm, order):
     wave = pad_last(order.wave(np.arange(share), frames), share_pad).transpose(0, 2, 1)
-    high, low = split_table(wave, 1)
+    high, low = split_table(wave, 1, LOW_SCALE, COARSE_SCALE)
     sums = np.concatenate([wave[0].sum(axis=0), wave[1].sum(axis=0)])
     shift = order.wave(np.arange(n_tm) * share, frames).transpose(0, 2, 1)
     shift = np.concatenate([shift, shift], axis=2).reshape(2 * n_tm, 2 * order.pad)
@@ -108,20 +107,23 @@
     values = slab_ref[...]
     verts = values.shape[0]
     n_tm, n_grp, row_share, share_pad = code_ref.shape
-    mean = jnp.sum(values, axis=1, keepdims=True) * (1.0 / share)
-    offset = values - mean
-    top = jnp.max(jnp.abs(offset), axis=1, keepdims=True)
-    top_digits = split_digits(top)
-    mean_digits = split_digits(mean)
+    highest = jnp.max(values, axis=1, keepdims=True)
+    lowest = jnp.min(values, axis=1, keepdims=True)
+    middle_digits = split_digits((highest + lowest) * 0.5)
+    middle = join_digits(*middle_digits)
+    offset = values - middle
+    top_digits = split_digits(jnp.maximum(highest - middle, middle - lowest))
     step = join_digits(*top_digits) * (1.0 / CODE_TOP)
     inverse = jnp.where(step > 0.0, 1.0 / jnp.where(step > 0.0, step, 1.0), 0.0)
     codes = jnp.clip(jnp.round(offset * inverse), -CODE_TOP, CODE_TOP).astype(jnp.int32)
     codes = jnp.concatenate(
         [codes, jnp.zeros((verts, share_pad - share), jnp.int32)], axis=1
     )
-    lane = lax.broadcasted_iota(jnp.int32, (verts, share_pad), 1) - share
-    for place, digit in enumerate(top_digits + mean_digits):
-        codes = jnp.where(lane == place, digit, codes)
+    edge = share_pad - LANES
+    tail = codes[:, edge:]
+    lane = lax.broadcasted_iota(jnp.int32, (verts, LANES), 1) + (edge - share)
+    for place, digit in enumerate(top_digits + middle_digits):
+        tail = jnp.where(lane == place, digit, tail)
 
     surr, freq_share = phase_ref.shape
     chunks = phase_chunks(freq_share, rows)
@@ -143,8 +145,7 @@
     place = jnp.where(lax.axis_index("lane") == 0, group, n_grp - 1 - group)
     phase = pltpu.roll(phase, rows - place * row_share, 1).T[:row_share]
     phase = jnp.concatenate([phase.astype(jnp.int32)] * n_tm, axis=0)
-    edge = share_pad - LANES
-    codes = jnp.concatenate([codes[:, :edge], codes[:, edge:] + phase], axis=1)
+    codes = jnp.concatenate([codes[:, :edge], tail + phase], axis=1)
     for m in range(n_tm):
         block = codes[m * row_share : (m + 1) * row_share].astype(jnp.int16)
         for g in range(n_grp):
@@ -189,16 +190,20 @@
         values = series[j].astype(jnp.float32)
         centered = values - jnp.sum(values, axis=0, keepdims=True) * (1.0 / frames)
         total = jnp.sum(centered * centered, axis=0, keepdims=True)
-        normed = (centered * lax.rsqrt(total + EPSILON)).astype(jnp.bfloat16).astype(jnp.float32)
-        first, second = normed[:half], normed[half:]
-        for parity, part in enumerate((first + second, first - second)):
-            if half_pad > half:
-                part = jnp.concatenate([part, jnp.zeros((half_pad - half, TILE), jnp.float32)], axis=0)
-            rounded = part.astype(jnp.bfloat16)
-            rest = part - rounded.astype(jnp.float32)
+        normed = centered * (lax.rsqrt(total + EPSILON) * COL_SCALE)
+        first, second = (
+            jnp.concatenate([part, jnp.zeros((half_pad - half, TILE), jnp.float32)], axis=0).astype(
+                jnp.bfloat16
+            )
+            for part in (normed[:half], normed[half:])
+        )
+        for parity, other in enumerate((second, -second)):
+            rounded = first + other
+            added = rounded - first
+            rest = (first - (rounded - added)) + (other - added)
             normed_ref[parity] = rounded
-            coarse_ref[parity, pl.ds(0, half_pad), :] = (part * COL_SCALE).astype(FLOAT8)
-            coarse_ref[parity, pl.ds(half_pad, half_pad), :] = (rest * COL_REST_SCALE).astype(FLOAT8)
+            coarse_ref[parity, pl.ds(0, half_pad), :] = rounded.astype(FLOAT8)
+            coarse_ref[parity, pl.ds(half_pad, half_pad), :] = rest.astype(FLOAT8)
 
     tile_copies[0].wait()
     normalize(0)
@@ -216,7 +221,7 @@
             rest = jnp.dot(
                 low[parity], coarse_refs[j % 2][parity], preferred_element_type=jnp.float32
             )
-            sums = (sums + rest * (1.0 / (LOW_SCALE * COL_SCALE))).astype(jnp.bfloat16)
+            sums = (sums + rest).astype(jnp.bfloat16)
             for q in range(2):
                 span = pl.ds(q * freq_pad + parity * freq_half, freq_half)
                 out[j, span, :] = sums[q * freq_half : (q + 1) * freq_half]
@@ -276,7 +281,7 @@
         rot_imag = spec_cos * sin_row - spec_sin * cos_row
         at_last = rot_real[:, block : block + LANES]
         energy = common + jnp.sum(at_last * at_last * last, axis=1, keepdims=True)
-        scale_ref[:, s : s + 1] = lax.rsqrt(energy + EPSILON) * math.sqrt(frames)
+        scale_ref[:, s : s + 1] = lax.rsqrt(energy + EPSILON) * (math.sqrt(frames) / COL_SCALE**2)
         span = pl.ds(s * rows, rows)
         rot_ref[span, :freq_pad] = rot_real.astype(jnp.bfloat16)
         rot_ref[span, freq_pad:] = (-rot_imag).astype(jnp.bfloat16)
@@ -307,7 +312,7 @@
     upper = upper.astype(jnp.bfloat16)
     digits = [codes[:, share + p : share + p + 1] for p in range(6)]
     step = join_digits(*digits[:3]) * (1.0 / CODE_TOP)
-    mean = join_digits(*digits[3:])
+    middle = join_digits(*digits[3:])
     surr = turn_ref.shape[0] // 2
     chunks = phase_chunks(freq_share, rows)
     above = phase_lane(share) % LANES
@@ -324,7 +329,7 @@
         wait_all(copies[q])
         part = jnp.dot(upper, high[q], preferred_element_type=jnp.float32)
         part += jnp.dot(coarse, low[q], preferred_element_type=jnp.float32) * (1.0 / COARSE_SCALE)
-        part = part * step + mean * shift_ref[0:1, q * freq_pad : (q + 1) * freq_pad]
+        part = part * step + middle * shift_ref[0:1, q * freq_pad : (q + 1) * freq_pad]
         if n_tm == 2:
             sign = shift_ref[2:3, :freq_pad]
             spec_ref[:, q * freq_pad : (q + 1) * freq_pad] = part[:rows] + part[rows:] * sign

time: 45 us -> 44.6 us (level)
  no operation moved by 1% of the time
where the time goes in v4:
time: 44.6 us; the launch traced here: 44.3 us
  Pallas kernels  21 us (47%)
  starting transfers between devices  14.8 us (33%)
  waiting for transfers between devices  6.16 us (14%)
  local copies, waits for them, and re-layouts  0.98 us (2%)
  between operations  0.76 us (2%)
  other arithmetic  0.57 us (1%)
    pallas_call x1, Pallas kernels, body(): pl.pallas_call(column_kernel, out_shape=pltpu.HBM((n_tiles, points, TILE)...  9.97 us
    all_to_all x1, starting transfers between devices, body(): lax.all_to_all(codes, ('grp', 'lane', 'tm'), 0, 0, tiled=True, axis_index...  8.31 us
    all_to_all x1, waiting for transfers between devices, body(): every = lax.all_to_all(best, ('grp', 'lane', 'tm'), 0, 0, tiled=True)  6.15 us
    all_to_all x1, starting transfers between devices, body(): every = lax.all_to_all(best, ('grp', 'lane', 'tm'), 0, 0, tiled=True)  4.36 us
    pallas_call x1, Pallas kernels, body(): pl.pallas_call(functools.partial(first_score_kernel, frames, last_freq),...  3.18 us
    pallas_call x1, Pallas kernels, body(): pl.pallas_call(functools.partial(spectrum_kernel, share, frames, last_fre...  3.06 us
    pallas_call x1, Pallas kernels, body(): pl.pallas_call(functools.partial(second_score_kernel, frames, last_freq),...  3.05 us
    pallas_call x1, Pallas kernels, body(): pl.pallas_call(functools.partial(encode_kernel, share, rows), out_shape=p...  1.77 us
  transfers between devices with their start and end apart: 4, of which 1 were waited for; matrix products, arithmetic and copies ran while one was open for 2% of the time, Pallas kernels for 30%

profile of v4, /device:TPU:0, one launch (start us, length us, event | category | flops | bytes accessed | tf_op | source)
XLA Modules:
  0.0 44.3 jit_solution(285929636528295751)
XLA Ops:
  0.6 1.8 %shard_map.104 = s16[2,8,16,640]{3,2,1,0:T(8,128)(2,1)} custom-call(f32[32,600]{1,0:T(8,128)} %bitcast.12, s32[4,300]{1,0:T(4,128)} %phase_ref.1), custom_call_target="tpu_custom_call" | custom-call | tf_op jit(solution)/shard_map/pallas_call | solution.py:433
  2.4 8.3 %all-to-all-start = ((s16[16,16,640]{2,1,0:T(8,128)(2,1)}), s16[16,16,640]{2,1,0:T(8,128)(2,1)S(1)}, u32[]{:S(2)}, u32[]{:S(2)}) async-start(s16[16,16,640]{2,1,0:T(8,128)(2,1)} %bitcast.1), calls=%async_computation | async-start | bytes 655360 | tf_op jit(solution)/shard_map/all_to_all | solution.py:441
  10.7 0.0 copy-start
  10.7 10.0 %shard_map.105.cols_hbm = bf16[6,1280,256]{2,1,0:T(8,128)(2,1)} custom-call(bf16[1200,1536]{1,0:T(8,128)(2,1)} %series_hbm.1, bf16[2,608,640]{2,1,0:T(8,128)(2,1)} %constant.20.clone.high_hbm, f8e4m3fn[2,608,1280]{2,1,0:T(32,128)(4,1)} %constant.21.clone.low_hbm), custom_call_target="tpu_custom_call" | custom-call | flops 7077888000 | tf_op jit(solution)/shard_map/pallas_call | solution.py:448
  20.7 0.0 all-to-all-done
  20.7 0.0 copy-done
  20.7 3.1 %shard_map.106 = (f32[128,1280]{1,0:T(8,128)S(1)}, f32[8,640]{1,0:T(8,128)S(1)}, bf16[3,1280,256]{2,1,0:T(8,128)(2,1)S(1)}) custom-call(s16[2,128,640]{2,1,0:T(8,128)(2,1)S(1)} %bitcast.10, bf16[2,640,640]{2,1,0:T(8,128)(2,1)} %constant.22.clone.high_hbm, f8e4m3fn[2,1280,640]{2,1,0:T(32,128)(4,1)} %constant.23.clone.low_hbm, ...), custom_call_target="tpu_custom_call" | custom-call | flops 838860800 | tf_op jit(solution)/shard_map/pallas_call | solution.py:473
  23.8 0.6 %collective-permute-start = (f32[128,1280]{1,0:T(8,128)S(1)}, f32[128,1280]{1,0:T(8,128)S(1)}, u32[]{:S(2)}, u32[]{:S(2)}) collective-permute-start(f32[128,1280]{1,0:T(8,128)S(1)} %get-tuple-element.13.spec_ref), channel_id=1, source_target_pairs={{0,2},{2,0},{1,3},{3,1},{4,6},{6,4},{5,7},{7,5},{8,10},{10,8},{9,1... | collective-permute-start | bytes 1966088 | tf_op jit(solution)/shard_map/ppermute | solution.py:496
  24.4 3.2 %shard_map.107 = (f32[4,128]{1,0:T(4,128)S(1)}, bf16[3,1280,256]{2,1,0:T(8,128)(2,1)S(1)}) custom-call(f32[128,1280]{1,0:T(8,128)S(1)} %get-tuple-element.13.spec_ref, f32[8,640]{1,0:T(8,128)S(1)} %get-tuple-element.14.turn_ref, bf16[3,1280,256]{2,1,0:T(8,128)(2,1)S(1)} %get-tuple-element.15.near_ref, bf16[6,1280,256]{2,1,0:T(8,128)(2,1)} %shard_map.105.cols_hbm), custom_call_target="tpu_custom_call" | custom-call | flops 2013265920 | tf_op jit(solution)/shard_map/pallas_call | solution.py:500
  27.6 0.0 collective-permute-done.spec_ref
  27.6 3.1 %shard_map.108 = (f32[2,4,128]{2,1,0:T(4,128)S(1)}, f32[32,1,128]{2,1,0:T(1,128)}) custom-call(f32[128,1280]{1,0:T(8,128)S(1)} %collective-permute-done.spec_ref, f32[8,640]{1,0:T(8,128)S(1)} %get-tuple-element.14.turn_ref, bf16[3,1280,256]{2,1,0:T(8,128)(2,1)S(1)} %get-tuple-element.15.near_ref, bf16[3,1280,256]{2,1,0:T(8,128)(2,1)S(1)} %get-tuple-element.16.far_ref, ...), custom_call_target="tpu_custom_call" | custom-call | flops 2013265920 | tf_op jit(solution)/shard_map/pallas_call | solution.py:513
  30.7 1.5 %collective-permute-start.1 = (f32[2,4,128]{2,1,0:T(4,128)S(1)}, f32[2,4,128]{2,1,0:T(4,128)S(1)}, u32[]{:S(2)}, u32[]{:S(2)}) collective-permute-start(f32[2,4,128]{2,1,0:T(4,128)S(1)} %get-tuple-element.18), channel_id=1, source_target_pairs={{0,1},{1,0},{2,3},{3,2},{4,5},{5,4},{6,7},{7,6},{8,9},{9,8},{10,11... | collective-permute-start | bytes 12296 | tf_op jit(solution)/shard_map/ppermute | solution.py:403
  32.2 4.4 %all-to-all-start.1 = ((f32[32,1,128]{2,1,0:T(1,128)}), f32[32,1,128]{2,1,0:T(1,128)S(1)}, u32[]{:S(2)}, u32[]{:S(2)}) async-start(f32[32,1,128]{2,1,0:T(1,128)} %get-tuple-element.19), calls=%async_computation.1 | async-start | bytes 32768 | tf_op jit(solution)/shard_map/all_to_all | solution.py:525
  36.6 0.0 collective-permute-done.1
  36.6 0.1 stack.9
  36.7 0.1 stack.10
  36.8 0.1 copy.11
  36.9 0.7 %reshape.20 = f32[4,512,1]{1,2,0:T(1,128)} reshape(f32[4,8,2,2,16]{4,3,2,1,0:T(2,128)S(1)} %copy.11) | data formatting | bytes 16384 | tf_op jit(solution)/shard_map/reshape | solution.py:530
  37.6 6.2 %all-to-all-done.1 = f32[32,1,128]{2,1,0:T(1,128)S(1)} async-done(((f32[32,1,128]{2,1,0:T(1,128)}), f32[32,1,128]{2,1,0:T(1,128)S(1)}, u32[]{:S(2)}, u32[]{:S(2)}) %all-to-all-start.1) | async-done | bytes 16416 | tf_op jit(solution)/shard_map/all_to_all | solution.py:525
  43.8 0.6 %reduce_max.9 = f32[128]{0:T(128)} reduce(f32[32,1,128]{2,1,0:T(1,128)S(1)} %all-to-all-done.1, f32[]{:T(128)} %constant.8.clone.1), dimensions={0,1}, to_apply=%region_0.0 | reduce | flops 3968 | bytes 16900 | tf_op jit(solution)/shard_map/reduce_max | solution.py:526
  (6 shorter events, 0.0 us)
Async XLA Ops:
  2.4 18.3 %all-to-all-start = ((s16[16,16,640]{2,1,0:T(8,128)(2,1)}), s16[16,16,640]{2,1,0:T(8,128)(2,1)S(1)}, u32[]{:S(2)}, u32[]{:S(2)}) async-start(s16[16,16,640]{2,1,0:T(8,128)(2,1)} %bitcast.1), calls=%async_computation | async-start | bytes 655360 | tf_op jit(solution)/shard_map/all_to_all | solution.py:441
  10.7 10.0 %copy-start = (f32[5,1280]{1,0:T(8,128)S(1)}, f32[5,1280]{1,0:T(8,128)}, u32[]{:S(2)}) copy-start(f32[5,1280]{1,0:T(8,128)} %constant.24.clone.shift_ref) | copy-start | bytes 76804
  23.8 3.8 %collective-permute-start = (f32[128,1280]{1,0:T(8,128)S(1)}, f32[128,1280]{1,0:T(8,128)S(1)}, u32[]{:S(2)}, u32[]{:S(2)}) collective-permute-start(f32[128,1280]{1,0:T(8,128)S(1)} %get-tuple-element.13.spec_ref), channel_id=1, source_target_pairs={{0,2},{2,0},{1,3},{3,1},{4,6},{6,4},{5,7},{7,5},{8,10},{10,8},{9,1... | collective-permute-start | bytes 1966088 | tf_op jit(solution)/shard_map/ppermute | solution.py:496
  30.7 5.9 %collective-permute-start.1 = (f32[2,4,128]{2,1,0:T(4,128)S(1)}, f32[2,4,128]{2,1,0:T(4,128)S(1)}, u32[]{:S(2)}, u32[]{:S(2)}) collective-permute-start(f32[2,4,128]{2,1,0:T(4,128)S(1)} %get-tuple-element.18), channel_id=1, source_target_pairs={{0,1},{1,0},{2,3},{3,2},{4,5},{5,4},{6,7},{7,6},{8,9},{9,8},{10,11... | collective-permute-start | bytes 12296 | tf_op jit(solution)/shard_map/ppermute | solution.py:403
  32.2 11.6 %all-to-all-start.1 = ((f32[32,1,128]{2,1,0:T(1,128)}), f32[32,1,128]{2,1,0:T(1,128)S(1)}, u32[]{:S(2)}, u32[]{:S(2)}) async-start(f32[32,1,128]{2,1,0:T(1,128)} %get-tuple-element.19), calls=%async_computation.1 | async-start | bytes 32768 | tf_op jit(solution)/shard_map/all_to_all | solution.py:525

commit v5 on v4

--- a/solution.py
+++ b/solution.py
@@ -209,6 +209,10 @@
     normalize(0)
     wait_all(table_copies + tile_copies[1:2])
     stores = []
+    if gap:
+        for q in range(2):
+            span = pl.ds(q * freq_pad + 2 * freq_half, gap)
+            out[:, span, :] = jnp.zeros((n_tiles, gap, TILE), jnp.bfloat16)
     for j in range(n_tiles):
         if j == 1:
             wait_all(tile_copies[2:])
@@ -225,11 +229,13 @@
             for q in range(2):
                 span = pl.ds(q * freq_pad + parity * freq_half, freq_half)
                 out[j, span, :] = sums[q * freq_half : (q + 1) * freq_half]
-        for q in range(2):
-            if gap:
-                span = pl.ds(q * freq_pad + 2 * freq_half, gap)
-                out[j, span, :] = jnp.zeros((gap, TILE), jnp.bfloat16)
-        stores.append(start_copy(out.at[j], out_hbm.at[j], store_sems.at[j]))
+                if j + 1 == n_tiles:
+                    start = q * freq_pad + parity * freq_half
+                    part = pl.ds(start, freq_half + parity * gap)
+                    place = n_tiles - 1 + 2 * parity + q
+                    stores.append(start_copy(out.at[j, part], out_hbm.at[j, part], store_sems.at[place]))
+        if j + 1 < n_tiles:
+            stores.append(start_copy(out.at[j], out_hbm.at[j], store_sems.at[j]))
     wait_all(stores)
 
 
@@ -295,7 +301,6 @@
 ):
     n_tm, rows, share_pad = codes_ref.shape
     freq_pad = high.shape[2]
-    place_copy = start_copy(place_hbm, place, sems.at[4])
     copies = [
         [
             start_copy(high_hbm.at[q], high.at[q], sems.at[2 * q]),
@@ -303,6 +308,7 @@
         ]
         for q in range(2)
     ]
+    place_copy = start_copy(place_hbm, place, sems.at[4])
     cols_copy = start_copy(cols_hbm.at[pl.ds(0, cols_ref.shape[0])], cols_ref, sems.at[5])
     codes = codes_ref[...].reshape(n_tm * rows, share_pad).astype(jnp.int32)
     upper = ((codes + 128) >> 8) << 8
@@ -322,11 +328,9 @@
         block = block[above : above + round_up(chunks * surr, 8)].astype(jnp.int32)
         parts = [block[c * surr : (c + 1) * surr] for c in range(chunks)]
         phases.append(jnp.concatenate(parts, axis=1))
-    place_copy.wait()
-    turn_cos, turn_sin = surrogate_turns(frames, last_freq, phases, place)
     parts = []
     for q in range(2):
-        wait_all(copies[q])
+        wait_all(copies[q] + [place_copy] * q)
         part = jnp.dot(upper, high[q], preferred_element_type=jnp.float32)
         part += jnp.dot(coarse, low[q], preferred_element_type=jnp.float32) * (1.0 / COARSE_SCALE)
         part = part * step + middle * shift_ref[0:1, q * freq_pad : (q + 1) * freq_pad]
@@ -345,6 +349,7 @@
             spec_sin += part_sin * shift_cos + part_cos * shift_sin
         spec_ref[:, :freq_pad] = spec_cos
         spec_ref[:, freq_pad:] = spec_sin
+    turn_cos, turn_sin = surrogate_turns(frames, last_freq, phases, place)
     turn_ref[pl.ds(0, surr), :] = turn_cos
     turn_ref[pl.ds(surr, surr), :] = turn_sin
     cols_copy.wait()
@@ -458,7 +463,7 @@
         ]
         + [pltpu.VMEM((2, half_pad, TILE), jnp.bfloat16)] * 2
         + [pltpu.VMEM((2, 2 * half_pad, TILE), FLOAT8)] * 2
-        + [pltpu.SemaphoreType.DMA((n_tiles + 2,)), pltpu.SemaphoreType.DMA((n_tiles,))],
+        + [pltpu.SemaphoreType.DMA((n_tiles + 2,)), pltpu.SemaphoreType.DMA((n_tiles + 3,))],
         compiler_params=limits,
         cost_estimate=pl.CostEstimate(
             flops=6 * order.pad * frames * columns, transcendentals=0, bytes_accessed=0

time: 44.6 us -> 44.5 us (level)
  no operation moved by 1% of the time
where the time goes in v5:
time: 44.5 us; the launch traced here: 44.2 us
  Pallas kernels  20.9 us (47%)
  starting transfers between devices  14.9 us (33%)
  waiting for transfers between devices  6.16 us (14%)
  local copies, waits for them, and re-layouts  0.98 us (2%)
  between operations  0.76 us (2%)
  other arithmetic  0.57 us (1%)
    pallas_call x1, Pallas kernels, body(): pl.pallas_call(column_kernel, out_shape=pltpu.HBM((n_tiles, points, TILE)...  9.88 us
    all_to_all x1, starting transfers between devices, body(): lax.all_to_all(codes, ('grp', 'lane', 'tm'), 0, 0, tiled=True, axis_index...  8.31 us
    all_to_all x1, waiting for transfers between devices, body(): every = lax.all_to_all(best, ('grp', 'lane', 'tm'), 0, 0, tiled=True)  6.15 us
    all_to_all x1, starting transfers between devices, body(): every = lax.all_to_all(best, ('grp', 'lane', 'tm'), 0, 0, tiled=True)  4.37 us
    pallas_call x1, Pallas kernels, body(): pl.pallas_call(functools.partial(first_score_kernel, frames, last_freq),...  3.19 us
    pallas_call x1, Pallas kernels, body(): pl.pallas_call(functools.partial(second_score_kernel, frames, last_freq),...  3.05 us
    pallas_call x1, Pallas kernels, body(): pl.pallas_call(functools.partial(spectrum_kernel, share, frames, last_fre...  2.97 us
    pallas_call x1, Pallas kernels, body(): pl.pallas_call(functools.partial(encode_kernel, share, rows), out_shape=p...  1.77 us
  transfers between devices with their start and end apart: 4, of which 1 were waited for; matrix products, arithmetic and copies ran while one was open for 2% of the time, Pallas kernels for 30%

profile of v5, /device:TPU:0, one launch (start us, length us, event | category | flops | bytes accessed | tf_op | source)
XLA Modules:
  0.0 44.2 jit_solution(786559812477882094)
XLA Ops:
  0.6 1.8 %shard_map.104 = s16[2,8,16,640]{3,2,1,0:T(8,128)(2,1)} custom-call(f32[32,600]{1,0:T(8,128)} %bitcast.12, s32[4,300]{1,0:T(4,128)} %phase_ref.1), custom_call_target="tpu_custom_call" | custom-call | tf_op jit(solution)/shard_map/pallas_call | solution.py:438
  2.4 8.3 %all-to-all-start = ((s16[16,16,640]{2,1,0:T(8,128)(2,1)}), s16[16,16,640]{2,1,0:T(8,128)(2,1)S(1)}, u32[]{:S(2)}, u32[]{:S(2)}) async-start(s16[16,16,640]{2,1,0:T(8,128)(2,1)} %bitcast.1), calls=%async_computation | async-start | bytes 655360 | tf_op jit(solution)/shard_map/all_to_all | solution.py:446
  10.7 0.0 copy-start
  10.7 9.9 %shard_map.105.cols_hbm = bf16[6,1280,256]{2,1,0:T(8,128)(2,1)} custom-call(bf16[1200,1536]{1,0:T(8,128)(2,1)} %series_hbm.1, bf16[2,608,640]{2,1,0:T(8,128)(2,1)} %constant.20.clone.high_hbm, f8e4m3fn[2,608,1280]{2,1,0:T(32,128)(4,1)} %constant.21.clone.low_hbm), custom_call_target="tpu_custom_call" | custom-call | flops 7077888000 | tf_op jit(solution)/shard_map/pallas_call | solution.py:453
  20.6 0.0 all-to-all-done
  20.6 0.0 copy-done
  20.6 3.0 %shard_map.106 = (f32[128,1280]{1,0:T(8,128)S(1)}, f32[8,640]{1,0:T(8,128)S(1)}, bf16[3,1280,256]{2,1,0:T(8,128)(2,1)S(1)}) custom-call(s16[2,128,640]{2,1,0:T(8,128)(2,1)S(1)} %bitcast.10, bf16[2,640,640]{2,1,0:T(8,128)(2,1)} %constant.22.clone.high_hbm, f8e4m3fn[2,1280,640]{2,1,0:T(32,128)(4,1)} %constant.23.clone.low_hbm, ...), custom_call_target="tpu_custom_call" | custom-call | flops 838860800 | tf_op jit(solution)/shard_map/pallas_call | solution.py:478
  23.6 0.6 %collective-permute-start = (f32[128,1280]{1,0:T(8,128)S(1)}, f32[128,1280]{1,0:T(8,128)S(1)}, u32[]{:S(2)}, u32[]{:S(2)}) collective-permute-start(f32[128,1280]{1,0:T(8,128)S(1)} %get-tuple-element.13.spec_ref), channel_id=1, source_target_pairs={{0,2},{2,0},{1,3},{3,1},{4,6},{6,4},{5,7},{7,5},{8,10},{10,8},{9,1... | collective-permute-start | bytes 1966088 | tf_op jit(solution)/shard_map/ppermute | solution.py:501
  24.3 3.2 %shard_map.107 = (f32[4,128]{1,0:T(4,128)S(1)}, bf16[3,1280,256]{2,1,0:T(8,128)(2,1)S(1)}) custom-call(f32[128,1280]{1,0:T(8,128)S(1)} %get-tuple-element.13.spec_ref, f32[8,640]{1,0:T(8,128)S(1)} %get-tuple-element.14.turn_ref, bf16[3,1280,256]{2,1,0:T(8,128)(2,1)S(1)} %get-tuple-element.15.near_ref, bf16[6,1280,256]{2,1,0:T(8,128)(2,1)} %shard_map.105.cols_hbm), custom_call_target="tpu_custom_call" | custom-call | flops 2013265920 | tf_op jit(solution)/shard_map/pallas_call | solution.py:505
  27.5 0.0 collective-permute-done.spec_ref
  27.5 3.1 %shard_map.108 = (f32[2,4,128]{2,1,0:T(4,128)S(1)}, f32[32,1,128]{2,1,0:T(1,128)}) custom-call(f32[128,1280]{1,0:T(8,128)S(1)} %collective-permute-done.spec_ref, f32[8,640]{1,0:T(8,128)S(1)} %get-tuple-element.14.turn_ref, bf16[3,1280,256]{2,1,0:T(8,128)(2,1)S(1)} %get-tuple-element.15.near_ref, bf16[3,1280,256]{2,1,0:T(8,128)(2,1)S(1)} %get-tuple-element.16.far_ref, ...), custom_call_target="tpu_custom_call" | custom-call | flops 2013265920 | tf_op jit(solution)/shard_map/pallas_call | solution.py:518
  30.5 1.5 %collective-permute-start.1 = (f32[2,4,128]{2,1,0:T(4,128)S(1)}, f32[2,4,128]{2,1,0:T(4,128)S(1)}, u32[]{:S(2)}, u32[]{:S(2)}) collective-permute-start(f32[2,4,128]{2,1,0:T(4,128)S(1)} %get-tuple-element.18), channel_id=1, source_target_pairs={{0,1},{1,0},{2,3},{3,2},{4,5},{5,4},{6,7},{7,6},{8,9},{9,8},{10,11... | collective-permute-start | bytes 12296 | tf_op jit(solution)/shard_map/ppermute | solution.py:408
  32.1 4.4 %all-to-all-start.1 = ((f32[32,1,128]{2,1,0:T(1,128)}), f32[32,1,128]{2,1,0:T(1,128)S(1)}, u32[]{:S(2)}, u32[]{:S(2)}) async-start(f32[32,1,128]{2,1,0:T(1,128)} %get-tuple-element.19), calls=%async_computation.1 | async-start | bytes 32768 | tf_op jit(solution)/shard_map/all_to_all | solution.py:530
  36.4 0.0 collective-permute-done.1
  36.5 0.1 stack.9
  36.5 0.1 stack.10
  36.7 0.1 copy.11
  36.7 0.7 %reshape.20 = f32[4,512,1]{1,2,0:T(1,128)} reshape(f32[4,8,2,2,16]{4,3,2,1,0:T(2,128)S(1)} %copy.11) | data formatting | bytes 16384 | tf_op jit(solution)/shard_map/reshape | solution.py:535
  37.5 6.2 %all-to-all-done.1 = f32[32,1,128]{2,1,0:T(1,128)S(1)} async-done(((f32[32,1,128]{2,1,0:T(1,128)}), f32[32,1,128]{2,1,0:T(1,128)S(1)}, u32[]{:S(2)}, u32[]{:S(2)}) %all-to-all-start.1) | async-done | bytes 16416 | tf_op jit(solution)/shard_map/all_to_all | solution.py:530
  43.6 0.6 %reduce_max.9 = f32[128]{0:T(128)} reduce(f32[32,1,128]{2,1,0:T(1,128)S(1)} %all-to-all-done.1, f32[]{:T(128)} %constant.8.clone.1), dimensions={0,1}, to_apply=%region_0.0 | reduce | flops 3968 | bytes 16900 | tf_op jit(solution)/shard_map/reduce_max | solution.py:531
  (6 shorter events, 0.0 us)
Async XLA Ops:
  2.4 18.2 %all-to-all-start = ((s16[16,16,640]{2,1,0:T(8,128)(2,1)}), s16[16,16,640]{2,1,0:T(8,128)(2,1)S(1)}, u32[]{:S(2)}, u32[]{:S(2)}) async-start(s16[16,16,640]{2,1,0:T(8,128)(2,1)} %bitcast.1), calls=%async_computation | async-start | bytes 655360 | tf_op jit(solution)/shard_map/all_to_all | solution.py:446
  10.7 9.9 %copy-start = (f32[5,1280]{1,0:T(8,128)S(1)}, f32[5,1280]{1,0:T(8,128)}, u32[]{:S(2)}) copy-start(f32[5,1280]{1,0:T(8,128)} %constant.24.clone.shift_ref) | copy-start | bytes 76804
  23.6 3.8 %collective-permute-start = (f32[128,1280]{1,0:T(8,128)S(1)}, f32[128,1280]{1,0:T(8,128)S(1)}, u32[]{:S(2)}, u32[]{:S(2)}) collective-permute-start(f32[128,1280]{1,0:T(8,128)S(1)} %get-tuple-element.13.spec_ref), channel_id=1, source_target_pairs={{0,2},{2,0},{1,3},{3,1},{4,6},{6,4},{5,7},{7,5},{8,10},{10,8},{9,1... | collective-permute-start | bytes 1966088 | tf_op jit(solution)/shard_map/ppermute | solution.py:501
  30.5 5.9 %collective-permute-start.1 = (f32[2,4,128]{2,1,0:T(4,128)S(1)}, f32[2,4,128]{2,1,0:T(4,128)S(1)}, u32[]{:S(2)}, u32[]{:S(2)}) collective-permute-start(f32[2,4,128]{2,1,0:T(4,128)S(1)} %get-tuple-element.18), channel_id=1, source_target_pairs={{0,1},{1,0},{2,3},{3,2},{4,5},{5,4},{6,7},{7,6},{8,9},{9,8},{10,11... | collective-permute-start | bytes 12296 | tf_op jit(solution)/shard_map/ppermute | solution.py:408
  32.1 11.6 %all-to-all-start.1 = ((f32[32,1,128]{2,1,0:T(1,128)}), f32[32,1,128]{2,1,0:T(1,128)S(1)}, u32[]{:S(2)}, u32[]{:S(2)}) async-start(f32[32,1,128]{2,1,0:T(1,128)} %get-tuple-element.19), calls=%async_computation.1 | async-start | bytes 32768 | tf_op jit(solution)/shard_map/all_to_all | solution.py:530

commit v6 on v5

--- a/solution.py
+++ b/solution.py
@@ -164,7 +164,7 @@
 
 
 def column_kernel(
-    series_hbm, high_hbm, low_hbm, out_hbm,
+    series_hbm, high_hbm, low_hbm, slab_low_hbm, out_hbm, slab_low_ref,
     series, high, low, out, normed_0, normed_1, coarse_0, coarse_1, load_sems, store_sems,
 ):
     n_tiles, frames, _ = series.shape
@@ -216,6 +216,7 @@
     for j in range(n_tiles):
         if j == 1:
             wait_all(tile_copies[2:])
+            slab_copy = start_copy(slab_low_hbm, slab_low_ref, load_sems.at[n_tiles + 2])
         if j + 1 < n_tiles:
             normalize(j + 1)
         for parity in range(2):
@@ -236,7 +237,7 @@
                     stores.append(start_copy(out.at[j, part], out_hbm.at[j, part], store_sems.at[place]))
         if j + 1 < n_tiles:
             stores.append(start_copy(out.at[j], out_hbm.at[j], store_sems.at[j]))
-    wait_all(stores)
+    wait_all([slab_copy] + stores)
 
 
 def surrogate_turns(frames, last_freq, phases, place_ref):
@@ -295,21 +296,15 @@
 
 def spectrum_kernel(
     share, frames, last_freq, freq_share,
-    codes_ref, high_hbm, low_hbm, place_hbm, cols_hbm, shift_ref,
+    codes_ref, low, high_hbm, place_hbm, cols_hbm, shift_ref,
     spec_ref, turn_ref, cols_ref,
-    high, low, place, sems,
+    high, place, sems,
 ):
     n_tm, rows, share_pad = codes_ref.shape
     freq_pad = high.shape[2]
-    copies = [
-        [
-            start_copy(high_hbm.at[q], high.at[q], sems.at[2 * q]),
-            start_copy(low_hbm.at[q], low.at[q], sems.at[1 + 2 * q]),
-        ]
-        for q in range(2)
-    ]
-    place_copy = start_copy(place_hbm, place, sems.at[4])
-    cols_copy = start_copy(cols_hbm.at[pl.ds(0, cols_ref.shape[0])], cols_ref, sems.at[5])
+    copies = [start_copy(high_hbm.at[q], high.at[q], sems.at[q]) for q in range(2)]
+    place_copy = start_copy(place_hbm, place, sems.at[2])
+    cols_copy = start_copy(cols_hbm.at[pl.ds(0, cols_ref.shape[0])], cols_ref, sems.at[3])
     codes = codes_ref[...].reshape(n_tm * rows, share_pad).astype(jnp.int32)
     upper = ((codes + 128) >> 8) << 8
     lower = (codes - upper).astype(jnp.float32)
@@ -330,7 +325,7 @@
         phases.append(jnp.concatenate(parts, axis=1))
     parts = []
     for q in range(2):
-        wait_all(copies[q] + [place_copy] * q)
+        wait_all([copies[q]] + [place_copy] * q)
         part = jnp.dot(upper, high[q], preferred_element_type=jnp.float32)
         part += jnp.dot(coarse, low[q], preferred_element_type=jnp.float32) * (1.0 / COARSE_SCALE)
         part = part * step + middle * shift_ref[0:1, q * freq_pad : (q + 1) * freq_pad]
@@ -450,11 +445,15 @@
 
     n_tiles = columns // TILE
     col_high, col_low = column_tables(frames, order)
-    cols = pl.pallas_call(
+    high, low, shift = slab_tables(frames, share, share_pad, n_tm, order)
+    cols, low = pl.pallas_call(
         column_kernel,
-        out_shape=pltpu.HBM((n_tiles, points, TILE), jnp.bfloat16),
-        in_specs=[HBM] * 3,
-        out_specs=HBM,
+        out_shape=(
+            pltpu.HBM((n_tiles, points, TILE), jnp.bfloat16),
+            pltpu.VMEM(low.shape, FLOAT8),
+        ),
+        in_specs=[HBM] * 4,
+        out_specs=(HBM, VMEM),
         scratch_shapes=[
             pltpu.VMEM((n_tiles, frames, TILE), jnp.bfloat16),
             pltpu.VMEM(col_high.shape, jnp.bfloat16),
@@ -463,15 +462,14 @@
         ]
         + [pltpu.VMEM((2, half_pad, TILE), jnp.bfloat16)] * 2
         + [pltpu.VMEM((2, 2 * half_pad, TILE), FLOAT8)] * 2
-        + [pltpu.SemaphoreType.DMA((n_tiles + 2,)), pltpu.SemaphoreType.DMA((n_tiles + 3,))],
+        + [pltpu.SemaphoreType.DMA((n_tiles + 3,)), pltpu.SemaphoreType.DMA((n_tiles + 3,))],
         compiler_params=limits,
         cost_estimate=pl.CostEstimate(
             flops=6 * order.pad * frames * columns, transcendentals=0, bytes_accessed=0
         ),
-    )(in_hbm(series), in_hbm(col_high), in_hbm(col_low))
+    )(in_hbm(series), in_hbm(col_high), in_hbm(col_low), in_hbm(low))
 
     received, cols = lax.optimization_barrier((received, cols))
-    high, low, shift = slab_tables(frames, share, share_pad, n_tm, order)
     place = placement(order, freqs, n_tm, rows)
     n_near = n_tiles // 2
     rot_shape = pltpu.VMEM((surr * rows, points), jnp.bfloat16)
@@ -482,13 +480,12 @@
             jax.ShapeDtypeStruct((2 * surr, order.pad), jnp.float32),
             pltpu.VMEM((n_near, points, TILE), jnp.bfloat16),
         ),
-        in_specs=[VMEM] + [HBM] * 4 + [VMEM],
+        in_specs=[VMEM] * 2 + [HBM] * 3 + [VMEM],
         out_specs=(VMEM,) * 3,
         scratch_shapes=[
             pltpu.VMEM(high.shape, jnp.bfloat16),
-            pltpu.VMEM(low.shape, FLOAT8),
             pltpu.VMEM(place.shape, FLOAT8),
-            pltpu.SemaphoreType.DMA((6,)),
+            pltpu.SemaphoreType.DMA((4,)),
         ],
         compiler_params=limits,
         cost_estimate=pl.CostEstimate(
@@ -496,7 +493,7 @@
         ),
     )(
         received.reshape(n_tm, rows, share_pad),
-        in_hbm(high), in_hbm(low), in_hbm(place), in_hbm(cols), shift,
+        low, in_hbm(high), in_hbm(place), in_hbm(cols), shift,
     )
     other = lax.ppermute(spec, "lane", [(i, (i + 1) % n_lane) for i in range(n_lane)])
     score_cost = pl.CostEstimate(

time: 44.5 us -> 44.3 us (level)
  no operation moved by 1% of the time
where the time goes in v6:
time: 44.3 us; the launch traced here: 44 us
  Pallas kernels  20.7 us (47%)
  starting transfers between devices  14.8 us (33%)
  waiting for transfers between devices  6.15 us (14%)
  local copies, waits for them, and re-layouts  0.98 us (2%)
  between operations  0.76 us (2%)
  other arithmetic  0.57 us (1%)
    pallas_call x1, Pallas kernels, body(): pl.pallas_call(column_kernel, out_shape=(pltpu.HBM((n_tiles, points, TILE...  9.89 us
    all_to_all x1, starting transfers between devices, body(): lax.all_to_all(codes, ('grp', 'lane', 'tm'), 0, 0, tiled=True, axis_index...  8.31 us
    all_to_all x1, waiting for transfers between devices, body(): every = lax.all_to_all(best, ('grp', 'lane', 'tm'), 0, 0, tiled=True)  6.14 us
    all_to_all x1, starting transfers between devices, body(): every = lax.all_to_all(best, ('grp', 'lane', 'tm'), 0, 0, tiled=True)  4.36 us
    pallas_call x1, Pallas kernels, body(): pl.pallas_call(functools.partial(first_score_kernel, frames, last_freq),...  3.21 us
    pallas_call x1, Pallas kernels, body(): pl.pallas_call(functools.partial(second_score_kernel, frames, last_freq),...  3.09 us
    pallas_call x1, Pallas kernels, body(): pl.pallas_call(functools.partial(spectrum_kernel, share, frames, last_fre...  2.71 us
    pallas_call x1, Pallas kernels, body(): pl.pallas_call(functools.partial(encode_kernel, share, rows), out_shape=p...  1.77 us
  transfers between devices with their start and end apart: 4, of which 1 were waited for; matrix products, arithmetic and copies ran while one was open for 2% of the time, Pallas kernels for 30%

profile of v6, /device:TPU:0, one launch (start us, length us, event | category | flops | bytes accessed | tf_op | source)
XLA Modules:
  0.0 44.0 jit_solution(7179486358337846678)
XLA Ops:
  0.6 1.8 %shard_map.104 = s16[2,8,16,640]{3,2,1,0:T(8,128)(2,1)} custom-call(f32[32,600]{1,0:T(8,128)} %bitcast.12, s32[4,300]{1,0:T(4,128)} %phase_ref.1), custom_call_target="tpu_custom_call" | custom-call | tf_op jit(solution)/shard_map/pallas_call | solution.py:433
  2.4 8.3 %all-to-all-start = ((s16[16,16,640]{2,1,0:T(8,128)(2,1)}), s16[16,16,640]{2,1,0:T(8,128)(2,1)S(1)}, u32[]{:S(2)}, u32[]{:S(2)}) async-start(s16[16,16,640]{2,1,0:T(8,128)(2,1)} %bitcast.1), calls=%async_computation | async-start | bytes 655360 | tf_op jit(solution)/shard_map/all_to_all | solution.py:441
  10.7 0.0 copy-start
  10.7 9.9 %shard_map.105 = (bf16[6,1280,256]{2,1,0:T(8,128)(2,1)}, f8e4m3fn[2,1280,640]{2,1,0:T(32,128)(4,1)S(1)}) custom-call(bf16[1200,1536]{1,0:T(8,128)(2,1)} %series_hbm.1, bf16[2,608,640]{2,1,0:T(8,128)(2,1)} %constant.20.clone.high_hbm, f8e4m3fn[2,608,1280]{2,1,0:T(32,128)(4,1)} %constant.21.clone.low_hbm, f8e4m3fn[2,1280,640]{2,1,0:T(32,128)(4,1)} %constant.23.clone.slab_low_hbm), custom_call_target="tpu_custom_call" | custom-call | flops 7077888000 | tf_op jit(solution)/shard_map/pallas_call | solution.py:449
  20.6 0.0 all-to-all-done
  20.6 0.0 copy-done
  20.7 2.7 %shard_map.106 = (f32[128,1280]{1,0:T(8,128)S(1)}, f32[8,640]{1,0:T(8,128)S(1)}, bf16[3,1280,256]{2,1,0:T(8,128)(2,1)S(1)}) custom-call(s16[2,128,640]{2,1,0:T(8,128)(2,1)S(1)} %bitcast.10, f8e4m3fn[2,1280,640]{2,1,0:T(32,128)(4,1)S(1)} %get-tuple-element.15.low, bf16[2,640,640]{2,1,0:T(8,128)(2,1)} %constant.22.clone.high_hbm, ...), custom_call_target="tpu_custom_call" | custom-call | flops 838860800 | tf_op jit(solution)/shard_map/pallas_call | solution.py:476
  23.4 0.6 %collective-permute-start = (f32[128,1280]{1,0:T(8,128)S(1)}, f32[128,1280]{1,0:T(8,128)S(1)}, u32[]{:S(2)}, u32[]{:S(2)}) collective-permute-start(f32[128,1280]{1,0:T(8,128)S(1)} %get-tuple-element.17.spec_ref), channel_id=1, source_target_pairs={{0,2},{2,0},{1,3},{3,1},{4,6},{6,4},{5,7},{7,5},{8,10},{10,8},{9,1... | collective-permute-start | bytes 1966088 | tf_op jit(solution)/shard_map/ppermute | solution.py:498
  24.0 3.2 %shard_map.107 = (f32[4,128]{1,0:T(4,128)S(1)}, bf16[3,1280,256]{2,1,0:T(8,128)(2,1)S(1)}) custom-call(f32[128,1280]{1,0:T(8,128)S(1)} %get-tuple-element.17.spec_ref, f32[8,640]{1,0:T(8,128)S(1)} %get-tuple-element.18.turn_ref, bf16[3,1280,256]{2,1,0:T(8,128)(2,1)S(1)} %get-tuple-element.19.near_ref, bf16[6,1280,256]{2,1,0:T(8,128)(2,1)} %get-tuple-element.16.cols_hbm), custom_call_target="tpu_custom_call" | custom-call | flops 2013265920 | tf_op jit(solution)/shard_map/pallas_call | solution.py:502
  27.2 0.0 collective-permute-done.spec_ref
  27.2 3.1 %shard_map.108 = (f32[2,4,128]{2,1,0:T(4,128)S(1)}, f32[32,1,128]{2,1,0:T(1,128)}) custom-call(f32[128,1280]{1,0:T(8,128)S(1)} %collective-permute-done.spec_ref, f32[8,640]{1,0:T(8,128)S(1)} %get-tuple-element.18.turn_ref, bf16[3,1280,256]{2,1,0:T(8,128)(2,1)S(1)} %get-tuple-element.19.near_ref, bf16[3,1280,256]{2,1,0:T(8,128)(2,1)S(1)} %get-tuple-element.20.far_ref, ...), custom_call_target="tpu_custom_call" | custom-call | flops 2013265920 | tf_op jit(solution)/shard_map/pallas_call | solution.py:515
  30.3 1.5 %collective-permute-start.1 = (f32[2,4,128]{2,1,0:T(4,128)S(1)}, f32[2,4,128]{2,1,0:T(4,128)S(1)}, u32[]{:S(2)}, u32[]{:S(2)}) collective-permute-start(f32[2,4,128]{2,1,0:T(4,128)S(1)} %get-tuple-element.22), channel_id=1, source_target_pairs={{0,1},{1,0},{2,3},{3,2},{4,5},{5,4},{6,7},{7,6},{8,9},{9,8},{10,11... | collective-permute-start | bytes 12296 | tf_op jit(solution)/shard_map/ppermute | solution.py:403
  31.9 4.4 %all-to-all-start.1 = ((f32[32,1,128]{2,1,0:T(1,128)}), f32[32,1,128]{2,1,0:T(1,128)S(1)}, u32[]{:S(2)}, u32[]{:S(2)}) async-start(f32[32,1,128]{2,1,0:T(1,128)} %get-tuple-element.23), calls=%async_computation.1 | async-start | bytes 32768 | tf_op jit(solution)/shard_map/all_to_all | solution.py:527
  36.2 0.0 collective-permute-done.1
  36.3 0.1 stack.9
  36.3 0.1 stack.10
  36.5 0.1 copy.11
  36.5 0.7 %reshape.20 = f32[4,512,1]{1,2,0:T(1,128)} reshape(f32[4,8,2,2,16]{4,3,2,1,0:T(2,128)S(1)} %copy.11) | data formatting | bytes 16384 | tf_op jit(solution)/shard_map/reshape | solution.py:532
  37.3 6.1 %all-to-all-done.1 = f32[32,1,128]{2,1,0:T(1,128)S(1)} async-done(((f32[32,1,128]{2,1,0:T(1,128)}), f32[32,1,128]{2,1,0:T(1,128)S(1)}, u32[]{:S(2)}, u32[]{:S(2)}) %all-to-all-start.1) | async-done | bytes 16416 | tf_op jit(solution)/shard_map/all_to_all | solution.py:527
  43.4 0.6 %reduce_max.9 = f32[128]{0:T(128)} reduce(f32[32,1,128]{2,1,0:T(1,128)S(1)} %all-to-all-done.1, f32[]{:T(128)} %constant.8.clone.1), dimensions={0,1}, to_apply=%region_0.0 | reduce | flops 3968 | bytes 16900 | tf_op jit(solution)/shard_map/reduce_max | solution.py:528
  (6 shorter events, 0.0 us)
Async XLA Ops:
  2.4 18.2 %all-to-all-start = ((s16[16,16,640]{2,1,0:T(8,128)(2,1)}), s16[16,16,640]{2,1,0:T(8,128)(2,1)S(1)}, u32[]{:S(2)}, u32[]{:S(2)}) async-start(s16[16,16,640]{2,1,0:T(8,128)(2,1)} %bitcast.1), calls=%async_computation | async-start | bytes 655360 | tf_op jit(solution)/shard_map/all_to_all | solution.py:441
  10.7 9.9 %copy-start = (f32[5,1280]{1,0:T(8,128)S(1)}, f32[5,1280]{1,0:T(8,128)}, u32[]{:S(2)}) copy-start(f32[5,1280]{1,0:T(8,128)} %constant.24.clone.shift_ref) | copy-start | bytes 76804
  23.4 3.9 %collective-permute-start = (f32[128,1280]{1,0:T(8,128)S(1)}, f32[128,1280]{1,0:T(8,128)S(1)}, u32[]{:S(2)}, u32[]{:S(2)}) collective-permute-start(f32[128,1280]{1,0:T(8,128)S(1)} %get-tuple-element.17.spec_ref), channel_id=1, source_target_pairs={{0,2},{2,0},{1,3},{3,1},{4,6},{6,4},{5,7},{7,5},{8,10},{10,8},{9,1... | collective-permute-start | bytes 1966088 | tf_op jit(solution)/shard_map/ppermute | solution.py:498
  30.3 5.9 %collective-permute-start.1 = (f32[2,4,128]{2,1,0:T(4,128)S(1)}, f32[2,4,128]{2,1,0:T(4,128)S(1)}, u32[]{:S(2)}, u32[]{:S(2)}) collective-permute-start(f32[2,4,128]{2,1,0:T(4,128)S(1)} %get-tuple-element.22), channel_id=1, source_target_pairs={{0,1},{1,0},{2,3},{3,2},{4,5},{5,4},{6,7},{7,6},{8,9},{9,8},{10,11... | collective-permute-start | bytes 12296 | tf_op jit(solution)/shard_map/ppermute | solution.py:403
  31.9 11.6 %all-to-all-start.1 = ((f32[32,1,128]{2,1,0:T(1,128)}), f32[32,1,128]{2,1,0:T(1,128)S(1)}, u32[]{:S(2)}, u32[]{:S(2)}) async-start(f32[32,1,128]{2,1,0:T(1,128)} %get-tuple-element.23), calls=%async_computation.1 | async-start | bytes 32768 | tf_op jit(solution)/shard_map/all_to_all | solution.py:527
